TPU v7x, 128 devices: a whole 4x4x4 slice. The times are simulated.
128 devices in a mesh: dp: 4 (over z), expert: 8 (over y, core), tensor: 4 (over x).
Axes of the slice: x: 4, y: 4, z: 4, core: 2. Of those that a mesh axis runs over, the one named last changes fastest.
Arguments:
- layer_in: bfloat16 [2, 512, 4096], P(None, 'dp'), may hold values from -6 to 6
- conv_state: bfloat16 [512, 3, 4096], P('dp', None, ('expert', 'tensor')), may hold values from -6 to 6
- ssm_state: float32 [512, 16, 4096], P('dp', None, ('expert', 'tensor')), may hold values from -6 to 6
- proj_inner: bfloat16 [4096, 4096], P(None, ('expert', 'tensor')), may hold values from -0.09375 to 0.09375
- proj_gate: bfloat16 [4096, 4096], P(None, ('expert', 'tensor')), may hold values from -0.09375 to 0.09375
- conv_weight: float32 [4, 4096], P(None, ('expert', 'tensor')), may hold values from -3 to 3
- conv_bias: float32 [4096], P(('expert', 'tensor')), may hold values from -3 to 3
- delta_down: bfloat16 [4096, 256], P(('expert', 'tensor')), may hold values from -0.09375 to 0.09375
- state_proj: bfloat16 [2, 16, 4096], P(None, None, ('expert', 'tensor')), may hold values from -0.09375 to 0.09375
- delta_up: bfloat16 [256, 4096], P(None, ('expert', 'tensor')), may hold values from -0.375 to 0.375
- delta_bias: float32 [4096], P(('expert', 'tensor')), may hold values from -4 to -1
- decay_log: float32 [16, 4096], P(None, ('expert', 'tensor')), may hold values from 0 to 2.8
- skip_gain: float32 [4096], P(('expert', 'tensor')), may hold values from 0 to 2
- proj_out: bfloat16 [4096, 4096], P(('expert', 'tensor')), may hold values from -0.09375 to 0.09375
- expert_gate: bfloat16 [8, 8192, 4096], P('expert', ('dp', 'tensor')), may hold values from -0.09375 to 0.09375
- expert_up: bfloat16 [8, 8192, 4096], P('expert', ('dp', 'tensor')), may hold values from -0.09375 to 0.09375
- expert_down: bfloat16 [8, 8192, 4096], P('expert', ('dp', 'tensor')), may hold values from -0.0625 to 0.0625
- expert_ids: int32 [2, 512, 2], P(None, ('dp', 'expert', 'tensor')), may hold values from 0 to 7, all different within a row; in each aligned block of 4 rows (0 to 3, 4 to 7, ..., all dimensions but the last counted through in order) at most 2 rows name the same one
- route_weight: float32 [2, 512, 2], P(None, ('dp', 'expert', 'tensor')), may hold values from 0.2 to 1
Outputs:
- layer_out: bfloat16 [2, 512, 4096], P(None, ('dp', 'expert', 'tensor'))
- conv_final: bfloat16 [512, 3, 4096], P('dp', None, ('expert', 'tensor'))
- state_final: float32 [512, 16, 4096], P('dp', None, ('expert', 'tensor'))
Inputs may be any that keep to these rules, and one draw needn't show every extreme that they name: `expert_ids`: in each decode step the 4 rows of one device (aligned blocks along the rows) name each expert at most 2 times, and in some devices' rows some expert is named exactly 2 times; the 2 experts of a row differ.
All inputs are finite; a program needn't handle non-finite values.
Results may differ from a plain program's by a relative error of at most 0.023.
Values may be sent and summed in bfloat16 or wider, within the bound.
A program may use at most 128 MiB of HBM per device.

v0:
```python
import jax
import jax.numpy as jnp
from jax import lax
from jax.sharding import PartitionSpec as P


def rms_rows(values, eps):
    return values * lax.rsqrt(jnp.mean(values * values, axis=-1, keepdims=True) + eps)


def expert_part(portion, expert_gate, expert_up, expert_down):
    gate_proj = jnp.einsum(
        "sxcd,xfd->sxcf", portion, expert_gate, preferred_element_type=jnp.float32
    )
    up_proj = jnp.einsum("sxcd,xfd->sxcf", portion, expert_up, preferred_element_type=jnp.float32)
    activation = (jax.nn.silu(gate_proj) * up_proj).astype(jnp.bfloat16)
    return jnp.einsum("sxcf,xfd->sxcd", activation, expert_down, preferred_element_type=jnp.float32)


def mixer_step(x_step, conv_state, ssm_state, weights):
    (
        proj_inner,
        proj_gate,
        conv_weight,
        conv_bias,
        delta_down,
        state_proj,
        delta_up,
        delta_bias,
        decay_log,
        skip_gain,
        proj_out,
    ) = weights
    x_float = x_step.astype(jnp.float32)
    normed = rms_rows(x_float, 1e-06).astype(jnp.bfloat16)
    conv_input = jnp.dot(normed, proj_inner, preferred_element_type=jnp.float32).astype(
        jnp.bfloat16
    )
    gate_branch = jnp.dot(normed, proj_gate, preferred_element_type=jnp.float32)
    window = jnp.concatenate([conv_state, conv_input[:, None, :]], axis=1)
    conv_sum = conv_bias + jnp.sum(window.astype(jnp.float32) * conv_weight[None], axis=1)
    activated = jax.nn.silu(conv_sum).astype(jnp.bfloat16)
    delta_part = jnp.dot(activated, delta_down, preferred_element_type=jnp.float32)
    state_part = jnp.einsum(
        "gc,knc->gkn", activated, state_proj, preferred_element_type=jnp.float32
    )
    delta_low, state_inputs = (
        lax.psum(delta_part.astype(jnp.bfloat16), ("expert", "tensor")).astype(jnp.float32),
        lax.psum(state_part.astype(jnp.bfloat16), ("expert", "tensor")).astype(jnp.float32),
    )
    delta_normed = rms_rows(delta_low, 1e-06).astype(jnp.bfloat16)
    step_size = jax.nn.softplus(
        jnp.dot(delta_normed, delta_up, preferred_element_type=jnp.float32) + delta_bias
    )
    act_float = activated.astype(jnp.float32)
    decays = jnp.exp(-step_size[:, None, :] * jnp.exp(decay_log)[None])
    ssm_state = (
        decays * ssm_state
        + step_size[:, None, :] * state_inputs[:, 0, :, None] * act_float[:, None, :]
    )
    readout = jnp.sum(ssm_state * state_inputs[:, 1, :, None], axis=1)
    gated_out = ((readout + skip_gain * act_float) * jax.nn.silu(gate_branch)).astype(jnp.bfloat16)
    local_rows = gated_out.shape[0] // lax.axis_size(("expert", "tensor"))
    mixer_out = lax.psum_scatter(
        jnp.dot(gated_out, proj_out, preferred_element_type=jnp.float32).astype(jnp.bfloat16),
        ("expert", "tensor"),
        scatter_dimension=0,
        tiled=True,
    ).astype(jnp.float32)
    first_row = lax.axis_index(("expert", "tensor")) * local_rows
    own_rows = lax.dynamic_slice_in_dim(x_float, first_row, local_rows, 0)
    return (own_rows + mixer_out, window[:, 1:, :], ssm_state)


def expert_layer(
    residual, expert_ids, route_weight, slots_each, expert_gate, expert_up, expert_down
):
    row_count, top_count = expert_ids.shape
    width = residual.shape[1]
    local_experts = expert_gate.shape[0]
    owners = lax.axis_size("expert")
    experts = owners * local_experts
    expert_in = rms_rows(residual, 1e-06).astype(jnp.bfloat16)
    flat_ids = expert_ids.reshape(-1)
    one_hot = (flat_ids[:, None] == jnp.arange(experts, dtype=jnp.int32)[None, :]).astype(jnp.int32)
    before = jnp.cumsum(one_hot, axis=0) - one_hot
    position = jnp.sum(before * one_hot, axis=1)
    slot_index = flat_ids * slots_each + position
    assign_table = (
        jnp.arange(experts * slots_each, dtype=jnp.int32)[:, None] == slot_index[None, :]
    ).astype(jnp.bfloat16)
    row_table = jnp.sum(assign_table.reshape(experts * slots_each, row_count, top_count), axis=2)
    buffer = jnp.dot(row_table, expert_in, preferred_element_type=jnp.float32).astype(jnp.bfloat16)
    buffer = buffer.reshape(owners, local_experts, slots_each, width)
    dp_size = lax.axis_size("dp")
    tp_size = lax.axis_size("tensor")
    copies = jnp.broadcast_to(
        buffer[None, :, None], (dp_size, owners, tp_size, local_experts, slots_each, width)
    )
    copies = copies.reshape(dp_size * owners * tp_size, local_experts, slots_each, width)
    partial_value = expert_part(
        lax.all_to_all(copies, ("dp", "expert", "tensor"), split_axis=0, concat_axis=0, tiled=True),
        expert_gate,
        expert_up,
        expert_down,
    )
    returned = lax.all_to_all(
        partial_value.astype(jnp.bfloat16),
        ("dp", "expert", "tensor"),
        split_axis=0,
        concat_axis=0,
        tiled=True,
    ).astype(partial_value.dtype)
    summed = jnp.sum(
        returned.reshape(dp_size, owners, tp_size, local_experts, slots_each, width), axis=(0, 2)
    )
    results = summed.astype(jnp.bfloat16)
    flat_results = results.reshape(experts * slots_each, width)
    picked = lax.dot_general(
        assign_table, flat_results, (((0,), (0,)), ((), ())), preferred_element_type=jnp.float32
    )
    expert_sum = jnp.sum(
        picked.reshape(row_count, top_count, width) * route_weight[:, :, None], axis=1
    )
    return (residual + expert_sum).astype(jnp.bfloat16)


def shards(
    layer_in,
    conv_state,
    ssm_state,
    proj_inner,
    proj_gate,
    conv_weight,
    conv_bias,
    delta_down,
    state_proj,
    delta_up,
    delta_bias,
    decay_log,
    skip_gain,
    proj_out,
    expert_gate,
    expert_up,
    expert_down,
    expert_ids,
    route_weight,
):
    weights = (
        proj_inner,
        proj_gate,
        conv_weight,
        conv_bias,
        delta_down,
        state_proj,
        delta_up,
        delta_bias,
        decay_log,
        skip_gain,
        proj_out,
    )
    step_count = layer_in.shape[0]
    row_dev = expert_ids.shape[1]
    capacity = row_dev // 2
    outputs = []
    for decode in range(step_count):
        residual, conv_state, ssm_state = mixer_step(
            layer_in[decode], conv_state, ssm_state, weights
        )
        outputs.append(
            expert_layer(
                residual,
                expert_ids[decode],
                route_weight[decode],
                capacity,
                expert_gate,
                expert_up,
                expert_down,
            )
        )
    layer_out = jnp.stack(outputs)
    return (layer_out, conv_state, ssm_state)


def solution(mesh):
    placed = (
        P(None, "dp", None),
        P("dp", None, ("expert", "tensor")),
        P("dp", None, ("expert", "tensor")),
        P(None, ("expert", "tensor")),
        P(None, ("expert", "tensor")),
        P(None, ("expert", "tensor")),
        P(("expert", "tensor")),
        P(("expert", "tensor"), None),
        P(None, None, ("expert", "tensor")),
        P(None, ("expert", "tensor")),
        P(("expert", "tensor")),
        P(None, ("expert", "tensor")),
        P(("expert", "tensor")),
        P(("expert", "tensor"), None),
        P("expert", ("dp", "tensor"), None),
        P("expert", ("dp", "tensor"), None),
        P("expert", ("dp", "tensor"), None),
        P(None, ("dp", "expert", "tensor"), None),
        P(None, ("dp", "expert", "tensor"), None),
    )
    return jax.shard_map(
        shards,
        mesh=mesh,
        in_specs=placed,
        out_specs=(
            P(None, ("dp", "expert", "tensor"), None),
            P("dp", None, ("expert", "tensor")),
            P("dp", None, ("expert", "tensor")),
        ),
        check_vma=False,
    )
```

profile of v0, /device:TPU:1, one launch (start us, length us, event | category | flops | bytes accessed | tf_op | source)
XLA Modules:
  0.0 435.3 jit_solution(13896383471634803210)
XLA Ops:
  7.2 2.2 fusion.18
  10.0 1.7 fusion.76
  12.5 0.7 fusion.154
  13.1 0.8 convolution_convert_fusion.6
  13.9 0.8 convolution_convert_fusion.7
  15.1 125.0 %all-reduce.2 = (bf16[128,2,16]{0,2,1:T(8,128)(2,1)S(1)}, bf16[128,2,16]{0,2,1:T(8,128)(2,1)S(1)}) all-reduce(bf16[128,2,16]{0,2,1:T(8,128)(2,1)S(1)} %convolution_convert_fusion.10, bf16[128,2,16]{0,2,1:T(8,128)(2,1)S(1)} %convolution_convert_fusion.11), channel_id=1, replica_groups=mesh['dp'=4,'expert'=8,'tensor'=4] {'expert','tensor'}, use_global_device_ids=true, to_apply=%region_17.18 | all-reduce | flops 8192 | bytes 32768 | tf_op jit(solution)/shard_map/psum | solution.py:49
  142.4 0.7 copy.88
  143.1 0.7 copy.89
  143.8 0.7 copy.97
  144.5 0.7 copy.98
  145.3 0.7 exp.47
  146.0 0.9 fusion.104
  146.9 1.0 fusion.106
  147.9 1.1 fusion.157
  149.0 1.1 fusion.158
  150.2 4.2 multiply_reduce_fusion
  154.4 3.1 convolution_convert_fusion.3
  157.5 3.1 convolution_convert_fusion.2
  160.6 0.6 copy-done.9
  162.6 2.5 slice_convert_fusion.1
  165.0 104.5 %all-reduce.8.cloned.1.call-done = (bf16[128,4096]{1,0:T(8,128)(2,1)}, bf16[128,4096]{1,0:T(8,128)(2,1)}) async-done(((bf16[128,4096]{1,0:T(8,128)(2,1)}, bf16[128,4096]{1,0:T(8,128)(2,1)}), (bf16[128,4096]{1,0:T(8,128)(2,1)}, bf16[128,4096]{1,0:T(8,128)(2,1)})) %all-reduce.8.cloned.1.call-update) | async-done | bytes 2097168
  269.5 1.1 multiply_reduce_fusion.5
  270.6 1.2 convolution_convert_fusion.5
  271.9 3.4 broadcast_in_dim.18
  275.4 8.1 %all-to-all-start = ((bf16[128,1,2,4096]{3,2,1,0:T(2,128)(2,1)}), bf16[128,1,2,4096]{3,2,1,0:T(2,128)(2,1)S(1)}, u32[]{:S(2)}, u32[]{:S(2)}) async-start(bf16[128,1,2,4096]{3,2,1,0:T(2,128)(2,1)} %bitcast.7), calls=%async_computation | async-start | bytes 4194304 | tf_op jit(solution)/shard_map/all_to_all | solution.py:102
  283.5 1.1 multiply_reduce_fusion.4
  284.6 1.2 convolution_convert_fusion.4
  285.9 28.4 %all-to-all-done = bf16[128,1,2,4096]{3,2,1,0:T(2,128)(2,1)S(1)} async-done(((bf16[128,1,2,4096]{3,2,1,0:T(2,128)(2,1)}), bf16[128,1,2,4096]{3,2,1,0:T(2,128)(2,1)S(1)}, u32[]{:S(2)}, u32[]{:S(2)}) %all-to-all-start) | async-done | bytes 2097184 | tf_op jit(solution)/shard_map/all_to_all | solution.py:102
  314.3 3.5 broadcast_in_dim.22
  317.8 4.9 %all-to-all-start.2 = ((bf16[128,1,2,4096]{3,2,1,0:T(2,128)(2,1)}), bf16[128,1,2,4096]{3,2,1,0:T(2,128)(2,1)}, u32[]{:S(2)}, u32[]{:S(2)}) async-start(bf16[128,1,2,4096]{3,2,1,0:T(2,128)(2,1)} %bitcast.37), calls=%async_computation.2 | async-start | bytes 4194304 | tf_op jit(solution)/shard_map/all_to_all | solution.py:102
  322.7 5.9 %fusion.24 = f32[128,1,2,512]{3,0,2,1:T(8,128)} fusion(bf16[1,512,4096]{2,1,0:T(8,128)(2,1)} %param.33, bf16[128,1,2,4096]{3,2,1,0:T(2,128)(2,1)S(1)} %all-to-all-done), kind=kOutput, calls=%fused_computation.36 | convolution fusion | flops 1073741824 | bytes 6815744 | tf_op jit(solution)/shard_map/sxcd,xfd->sxcf/dot_general | solution.py:12
  328.6 9.0 %fusion = bf16[128,1,2,4096]{3,0,2,1:T(8,128)(2,1)} fusion(bf16[1,512,4096]{2,1,0:T(8,128)(2,1)} %param.35, bf16[1,512,4096]{2,1,0:T(8,128)(2,1)} %param.34, bf16[128,1,2,4096]{3,2,1,0:T(2,128)(2,1)S(1)} %all-to-all-done, f32[128,1,2,512]{3,0,2,1:T(8,128)} %fusion.24), kind=kOutput, calls=%fused_computation.2 | convolution fusion | flops 2149318656 | bytes 13107200 | tf_op jit(solution)/shard_map/sxcf,xfd->sxcd/dot_general | solution.py:17
  337.6 5.1 %copy.93 = bf16[128,1,2,4096]{3,2,1,0:T(2,128)(2,1)} copy(bf16[128,1,2,4096]{3,0,2,1:T(8,128)(2,1)} %fusion) | data formatting | bytes 4194304 | tf_op jit(solution)/shard_map/convert_element_type | solution.py:108
  342.7 10.6 %all-to-all-done.2 = bf16[128,1,2,4096]{3,2,1,0:T(2,128)(2,1)} async-done(((bf16[128,1,2,4096]{3,2,1,0:T(2,128)(2,1)}), bf16[128,1,2,4096]{3,2,1,0:T(2,128)(2,1)}, u32[]{:S(2)}, u32[]{:S(2)}) %all-to-all-start.2) | async-done | bytes 2097184 | tf_op jit(solution)/shard_map/all_to_all | solution.py:102
  353.3 3.8 all-to-all-start.1
  357.1 6.5 %fusion.29 = f32[128,1,2,512]{3,0,2,1:T(8,128)} fusion(bf16[1,512,4096]{2,1,0:T(8,128)(2,1)} %param.33, bf16[128,1,2,4096]{3,2,1,0:T(2,128)(2,1)} %all-to-all-done.2), kind=kOutput, calls=%fused_computation.37 | convolution fusion | flops 1073741824 | bytes 6815744 | tf_op jit(solution)/shard_map/sxcd,xfd->sxcf/dot_general | solution.py:12
  363.7 9.7 %fusion.1 = bf16[128,1,2,4096]{3,0,2,1:T(8,128)(2,1)} fusion(bf16[1,512,4096]{2,1,0:T(8,128)(2,1)} %param.35, bf16[1,512,4096]{2,1,0:T(8,128)(2,1)} %param.34, bf16[128,1,2,4096]{3,2,1,0:T(2,128)(2,1)} %all-to-all-done.2, f32[128,1,2,512]{3,0,2,1:T(8,128)} %fusion.29), kind=kOutput, calls=%fused_computation.3 | convolution fusion | flops 2149318656 | bytes 13107200 | tf_op jit(solution)/shard_map/sxcf,xfd->sxcd/dot_general | solution.py:17
  373.3 5.1 %copy.102 = bf16[128,1,2,4096]{3,2,1,0:T(2,128)(2,1)} copy(bf16[128,1,2,4096]{3,0,2,1:T(8,128)(2,1)} %fusion.1) | data formatting | bytes 4194304 | tf_op jit(solution)/shard_map/convert_element_type | solution.py:108
  378.5 9.6 %all-to-all-done.1 = bf16[128,1,2,4096]{3,2,1,0:T(2,128)(2,1)S(1)} async-done(((bf16[128,1,2,4096]{3,2,1,0:T(2,128)(2,1)}), bf16[128,1,2,4096]{3,2,1,0:T(2,128)(2,1)S(1)}, u32[]{:S(2)}, u32[]{:S(2)}) %all-to-all-start.1) | async-done | bytes 2097184 | tf_op jit(solution)/shard_map/all_to_all | solution.py:107
  388.1 1.3 copy-done.2
  389.5 3.9 all-to-all-start.3
  393.5 0.7 fusion.108
  394.2 3.8 reduce.4
  398.3 1.0 fusion.130
  399.3 25.0 %all-to-all-done.3 = bf16[128,1,2,4096]{3,2,1,0:T(2,128)(2,1)S(1)} async-done(((bf16[128,1,2,4096]{3,2,1,0:T(2,128)(2,1)}), bf16[128,1,2,4096]{3,2,1,0:T(2,128)(2,1)S(1)}, u32[]{:S(2)}, u32[]{:S(2)}) %all-to-all-start.3) | async-done | bytes 2097184 | tf_op jit(solution)/shard_map/all_to_all | solution.py:107
  424.3 2.3 reduce.5
  426.8 1.0 fusion.131
  427.8 0.7 pad_maximum_fusion.2
  (96 shorter events, 5.4 us)
Async XLA Ops:
  7.2 147.2 %copy-start = (bf16[128,4096]{1,0:T(8,128)(2,1)S(1)}, bf16[128,4096]{1,0:T(8,128)(2,1)}, u32[]{:S(2)}) copy-start(bf16[128,4096]{1,0:T(8,128)(2,1)} %param.32) | copy-start | bytes 3145732
  7.2 2.8 copy-start.1
  7.2 138.8 %all-reduce.10.cloned.1.call-start = ((), (), s32[]{:S(2)}) async-start(), calls=%async_computation.5 | async-start | bytes 262144 | tf_op jit(solution)/shard_map/psum | solution.py:48
  7.2 4.5 %copy-start.22 = (bf16[4096,128]{1,0:T(8,128)(2,1)S(1)}, bf16[4096,128]{1,0:T(8,128)(2,1)}, u32[]{:S(2)}) copy-start(bf16[4096,128]{1,0:T(8,128)(2,1)} %param.22) | copy-start | bytes 3145732
  9.4 0.5 copy-start.15
  9.5 2.8 copy-start.13
  10.0 2.3 copy-start.3
  11.7 0.7 copy-start.11
  11.7 0.7 copy-start.21
  11.7 1.4 copy-start.4
  11.8 3.0 copy-start.5
  11.8 128.3 %copy-start.6 = (s32[2,4,2]{1,2,0:T(2,128)S(1)}, s32[2,4,2]{1,2,0:T(2,128)}, u32[]{:S(2)}) copy-start(s32[2,4,2]{1,2,0:T(2,128)} %param.36) | copy-start | bytes 196
  14.7 254.8 %all-reduce.8.cloned.1.call-start = ((), (), s32[]{:S(2)}) async-start(), calls=%async_computation.4 | async-start | bytes 4194304
  140.6 0.6 copy-start.16
  141.3 3.2 copy-start.7
  141.6 8.6 %copy-start.18 = (s32[8]{0:T(128)}, s32[8]{0:T(128)S(1)}, u32[]{:S(2)}) copy-start(s32[8]{0:T(128)S(1)} %select_reduce_fusion.1) | copy-start | bytes 100
  154.3 3.1 copy-start.12
  154.4 3.1 copy-start.14
  160.6 0.7 copy-start.9
  160.6 0.7 copy-start.10
  160.6 0.7 copy-start.23
  275.4 38.9 %all-to-all-start = ((bf16[128,1,2,4096]{3,2,1,0:T(2,128)(2,1)}), bf16[128,1,2,4096]{3,2,1,0:T(2,128)(2,1)S(1)}, u32[]{:S(2)}, u32[]{:S(2)}) async-start(bf16[128,1,2,4096]{3,2,1,0:T(2,128)(2,1)} %bitcast.7), calls=%async_computation | async-start | bytes 4194304 | tf_op jit(solution)/shard_map/all_to_all | solution.py:102
  317.8 35.5 %all-to-all-start.2 = ((bf16[128,1,2,4096]{3,2,1,0:T(2,128)(2,1)}), bf16[128,1,2,4096]{3,2,1,0:T(2,128)(2,1)}, u32[]{:S(2)}, u32[]{:S(2)}) async-start(bf16[128,1,2,4096]{3,2,1,0:T(2,128)(2,1)} %bitcast.37), calls=%async_computation.2 | async-start | bytes 4194304 | tf_op jit(solution)/shard_map/all_to_all | solution.py:102
  353.3 34.8 %all-to-all-start.1 = ((bf16[128,1,2,4096]{3,2,1,0:T(2,128)(2,1)}), bf16[128,1,2,4096]{3,2,1,0:T(2,128)(2,1)S(1)}, u32[]{:S(2)}, u32[]{:S(2)}) async-start(bf16[128,1,2,4096]{3,2,1,0:T(2,128)(2,1)} %copy.93), calls=%async_computation.1 | async-start | bytes 4194304 | tf_op jit(solution)/shard_map/all_to_all | solution.py:107
  378.5 14.9 %copy-start.8 = (s32[8]{0:T(128)S(1)}, s32[8]{0:T(128)}, u32[]{:S(2)}) copy-start(s32[8]{0:T(128)} %copy-done.7) | copy-start | bytes 100
  378.5 14.9 %copy-start.19 = (s32[8]{0:T(128)S(1)}, s32[8]{0:T(128)}, u32[]{:S(2)}) copy-start(s32[8]{0:T(128)} %copy-done.18) | copy-start | bytes 100
  378.5 15.0 %copy-start.17 = (s32[8]{0:T(128)S(1)}, s32[8]{0:T(128)}, u32[]{:S(2)}) copy-start(s32[8]{0:T(128)} %copy-done.16) | copy-start | bytes 100
  378.5 15.7 %copy-start.20 = (f32[2,4,2]{1,2,0:T(2,128)S(1)}, f32[2,4,2]{1,2,0:T(2,128)}, u32[]{:S(2)}) copy-start(f32[2,4,2]{1,2,0:T(2,128)} %param.37) | copy-start | bytes 196
  388.1 1.3 copy-start.2
  389.5 34.8 %all-to-all-start.3 = ((bf16[128,1,2,4096]{3,2,1,0:T(2,128)(2,1)}), bf16[128,1,2,4096]{3,2,1,0:T(2,128)(2,1)S(1)}, u32[]{:S(2)}, u32[]{:S(2)}) async-start(bf16[128,1,2,4096]{3,2,1,0:T(2,128)(2,1)} %copy.102), calls=%async_computation.3 | async-start | bytes 4194304 | tf_op jit(solution)/shard_map/all_to_all | solution.py:107
Sparse Core Ops, SparseCore 0:
  14.8 103.5 all-reduce.9
  160.7 108.7 all-reduce.7
where the time goes:
time: 436 us; the launch traced here: 435 us
  waiting for transfers between devices  178 us (41%)
  blocking collectives  125 us (29%)
  matrix products  46.3 us (11%)
  local copies, waits for them, and re-layouts  25.4 us (6%)
  other arithmetic  24.6 us (6%)
  starting transfers between devices  20.8 us (5%)
  between operations  15.1 us (3%)
    psum x1, blocking collectives, mixer_step(): lax.psum(state_part.astype(jnp.bfloat16), ('expert', 'tensor'))  125 us
    unnamed x3, waiting for transfers between devices  105 us
    all_to_all x2, waiting for transfers between devices, expert_layer(): lax.all_to_all(copies, ('dp', 'expert', 'tensor'), split_axis=0, concat_a...  39 us
    all_to_all x2, waiting for transfers between devices, expert_layer(): lax.all_to_all(partial_value.astype(jnp.bfloat16), ('dp', 'expert', 'tens...  34.6 us
    dot_general x2, matrix products, expert_part(): jnp.einsum('sxcf,xfd->sxcd', activation, expert_down, preferred_element_t...  18.7 us
    all_to_all x2, starting transfers between devices, expert_layer(): lax.all_to_all(copies, ('dp', 'expert', 'tensor'), split_axis=0, concat_a...  13 us
    dot_general x2, matrix products, expert_part(): jnp.einsum('sxcd,xfd->sxcf', portion, expert_gate, preferred_element_type...  12.4 us
    convert_element_type x2, local copies, waits for them, and re-layouts, expert_layer(): partial_value.astype(jnp.bfloat16)  10.2 us
  transfers between devices with their start and end apart: 6, of which 5 were waited for; matrix products, arithmetic and copies ran while one was open for 13% of the time, Pallas kernels for 0%

commit v1 on v0

v1 whole, which is shorter than its diff:
```python
import functools

import jax
import jax.numpy as jnp
from jax import lax
from jax.experimental import pallas as pl
from jax.experimental.pallas import tpu as pltpu
from jax.sharding import PartitionSpec as P

MESH = pl.DeviceIdType.MESH
F32 = jnp.float32
BF16 = jnp.bfloat16
MIB = 2**20


def place():
    z, e, x = lax.axis_index("dp"), lax.axis_index("expert"), lax.axis_index("tensor")
    return z, lax.div(e, 2), lax.rem(e, 2), x


def remote(src, dst, sems, at, device):
    return pltpu.make_async_remote_copy(
        src_ref=src,
        dst_ref=dst,
        send_sem=sems[0].at[at],
        recv_sem=sems[1].at[at],
        device_id=device,
        device_id_type=MESH,
    )


def greet(devices):
    barrier = pltpu.get_barrier_semaphore()
    for device in devices:
        pl.semaphore_signal(barrier, inc=1, device_id=device, device_id_type=MESH)
    pl.semaphore_wait(barrier, len(devices))


def small_sum_kernel(part, out, recv, send_a, recv_a, send_b, recv_b):
    z, y, c, x = place()
    me = (y * 2 + c) * 4 + x

    def device(p):
        return (z, lax.div(p, 4), lax.rem(p, 4))

    barrier = pltpu.get_barrier_semaphore()

    def signal(i, carry):
        pl.semaphore_signal(
            barrier, inc=1, device_id=device(lax.rem(me + i, 32)), device_id_type=MESH
        )
        return carry

    lax.fori_loop(1, 32, signal, 0)
    pl.semaphore_wait(barrier, 31)

    def first(i):
        p = lax.rem(me + i, 32)
        return remote(part.at[p], recv.at[i - 1], (send_a, recv_a), i - 1, device(p))

    def start_first(i, carry):
        first(i).start()
        return carry

    lax.fori_loop(1, 32, start_first, 0)

    def add(i, total):
        first(i).wait()
        return total + recv[i - 1].astype(F32)

    total = lax.fori_loop(1, 32, add, part[me].astype(F32))
    low, state = total[:8], total[8:]
    normed = low * lax.rsqrt(jnp.mean(low * low, axis=-1, keepdims=True) + 1e-06)
    high = state.astype(BF16)
    rest = state - high.astype(F32)
    shifted = jnp.concatenate([high.astype(F32)[:, :32], rest[:, :32], state[:, 64:]], axis=1)
    out[me] = jnp.concatenate([normed, shifted], axis=0).astype(BF16)

    def second(i):
        p = lax.rem(me + i, 32)
        return remote(out.at[me], out.at[me], (send_b, recv_b), i - 1, device(p))

    def second_from(i):
        p = lax.rem(me + 32 - i, 32)
        return remote(out.at[p], out.at[p], (send_b, recv_b), i - 1, device(p))

    def start_second(i, carry):
        second(i).start()
        return carry

    lax.fori_loop(1, 32, start_second, 0)

    def wait_second(i, carry):
        second(i).wait_send()
        second_from(i).wait_recv()
        return carry

    lax.fori_loop(1, 32, wait_second, 0)


def small_sum(part):
    return pl.pallas_call(
        small_sum_kernel,
        out_shape=jax.ShapeDtypeStruct((32, 16, 256), BF16),
        in_specs=[pl.BlockSpec(memory_space=pltpu.VMEM)],
        out_specs=pl.BlockSpec(memory_space=pltpu.VMEM),
        scratch_shapes=[
            pltpu.VMEM((31, 16, 256), BF16),
            pltpu.SemaphoreType.DMA((31,)),
            pltpu.SemaphoreType.DMA((31,)),
            pltpu.SemaphoreType.DMA((31,)),
            pltpu.SemaphoreType.DMA((31,)),
        ],
        compiler_params=pltpu.CompilerParams(
            collective_id=0, has_side_effects=True, vmem_limit_bytes=16 * MIB
        ),
        name="small_sum",
    )(part)


def mixer_out_kernel(
    gated, weight, own, res, first, mine, got0, sum_a, sum_b, got1, mid, got2, last, got3, ss, rs
):
    z, y, c, x = place()
    sems = (ss, rs)

    def dev(dy=0, dc=0, dx=0):
        return (z, lax.rem(y + dy, 4) * 2 + lax.rem(c + dc, 2), lax.rem(x + dx, 4))

    greet([dev(dc=1)] + [dev(dx=d) for d in (1, 2, 3)] + [dev(dy=d) for d in (1, 2, 3)])
    other = 1 - c
    left = gated[...]
    swaps = []
    for q in range(2):
        cols = pl.ds(pl.multiple_of(other * 2048 + q * 1024, 1024), 1024)
        first[q] = jnp.dot(left, weight[:, cols], preferred_element_type=F32).astype(BF16)
        swap = remote(first.at[q], got0.at[q], sems, q, dev(dc=1))
        swap.start()
        swaps.append(swap)
    for q in range(2):
        cols = pl.ds(pl.multiple_of(c * 2048 + q * 1024, 1024), 1024)
        mine[q] = jnp.dot(left, weight[:, cols], preferred_element_type=F32)
    ones = []
    for q in range(2):
        swaps[q].wait()
        both = mine[q] + got0[q].astype(F32)
        mine[q] = both
        blocks = both.astype(BF16).reshape(4, 4, 16, 1024)
        if q == 0:
            for at in range(4):
                for to in range(4):
                    sum_a[to, at] = blocks[at, to]
        else:
            sum_b[...] = blocks
        for d in (1, 2, 3):
            if q == 0:
                copy = remote(
                    sum_a.at[lax.rem(x + d, 4)], got1.at[0, d - 1], sems, 2 + d - 1, dev(dx=d)
                )
            else:
                copy = remote(
                    sum_b.at[lax.rem(y + d, 4)], got1.at[1, d - 1], sems, 5 + d - 1, dev(dy=d)
                )
            copy.start()
            ones.append(copy)
    twos = []
    for q in range(2):
        for d in range(3):
            ones[q * 3 + d].wait()
        kept = sum_a[x] if q == 0 else sum_b[y]
        total = kept.astype(F32)
        for d in range(3):
            total = total + got1[q, d].astype(F32)
        mid[q] = total.astype(BF16)
        for d in (1, 2, 3):
            if q == 0:
                copy = remote(
                    mid.at[0, lax.rem(y + d, 4)], got2.at[0, d - 1], sems, 8 + d - 1, dev(dy=d)
                )
            else:
                copy = remote(
                    mid.at[1, lax.rem(x + d, 4)], got2.at[1, d - 1], sems, 11 + d - 1, dev(dx=d)
                )
            copy.start()
            twos.append(copy)
    for q in range(2):
        for d in range(3):
            twos[q * 3 + d].wait()
        total = (mid[0, y] if q == 0 else mid[1, x]).astype(F32)
        for d in range(3):
            total = total + got2[q, d].astype(F32)
        last[:, :, q * 1024 : (q + 1) * 1024] = total.reshape(2, 8, 1024)
    swap = remote(last.at[other], got3, sems, 14, dev(dc=1))
    swap.start()
    here = pl.ds(pl.multiple_of(c * 2048, 2048), 2048)
    there = pl.ds(pl.multiple_of(other * 2048, 2048), 2048)
    res[:, here] = last[c] + own[:, here].astype(F32)
    swap.wait()
    res[:, there] = got3[...] + own[:, there].astype(F32)


def mixer_out(gated, weight, own):
    return pl.pallas_call(
        mixer_out_kernel,
        out_shape=jax.ShapeDtypeStruct((8, 4096), F32),
        in_specs=[pl.BlockSpec(memory_space=pltpu.VMEM)] * 3,
        out_specs=pl.BlockSpec(memory_space=pltpu.VMEM),
        scratch_shapes=[
            pltpu.VMEM((2, 256, 1024), BF16),
            pltpu.VMEM((2, 256, 1024), F32),
            pltpu.VMEM((2, 256, 1024), BF16),
            pltpu.VMEM((4, 4, 16, 1024), BF16),
            pltpu.VMEM((4, 4, 16, 1024), BF16),
            pltpu.VMEM((2, 3, 4, 16, 1024), BF16),
            pltpu.VMEM((2, 4, 16, 1024), BF16),
            pltpu.VMEM((2, 3, 16, 1024), BF16),
            pltpu.VMEM((2, 8, 2048), F32),
            pltpu.VMEM((8, 2048), F32),
            pltpu.SemaphoreType.DMA((15,)),
            pltpu.SemaphoreType.DMA((15,)),
        ],
        compiler_params=pltpu.CompilerParams(
            collective_id=1, has_side_effects=True, vmem_limit_bytes=24 * MIB
        ),
        name="mixer_out",
    )(gated, weight, own)


GATHER = 14


def expert_kernel(
    res, spread, gather_perm, back_perm, mix_high, mix_low, gate_hbm, up_hbm, down_hbm,
    out,
    gate, up, down, message, arrived, rows, act, part, hop, hop2, got_hop, got_full, quad, got_quad,
    reply, returned, local, ss, rs,
):
    z, y, c, x = place()
    e = y * 2 + c
    sems = (ss, rs)
    loads = []
    for i, (a, b) in enumerate(((gate_hbm, gate), (up_hbm, up), (down_hbm, down))):
        load = pltpu.make_async_copy(a.at[0], b, local.at[i])
        load.start()
        loads.append(load)

    def dev_e(d):
        return (z, lax.rem(e + d, 8), x)

    def dev_x(d):
        return (z, e, lax.rem(x + d, 4))

    def dev_z(d):
        return (lax.rem(z + d, 4), e, x)

    residual = res[...]
    normed = residual * lax.rsqrt(jnp.mean(residual * residual, axis=-1, keepdims=True) + 1e-06)
    stacked = jnp.concatenate([normed[:, k * 512 : (k + 1) * 512] for k in range(8)], axis=0)
    spread_rows = jnp.dot(spread[...], stacked.astype(BF16), preferred_element_type=F32)
    message[...] = spread_rows.astype(BF16).reshape(2, 8, 16, 512)
    greet([dev_e(d) for d in range(1, 8)] + [f(d) for f in (dev_x, dev_z) for d in (1, 2, 3)])

    sends = {}
    for s in range(2):
        for d in range(1, 8):
            copy = remote(
                message.at[s, lax.rem(e + d, 8)],
                arrived.at[s, e],
                sems,
                s * 7 + d - 1,
                dev_e(d),
            )
            copy.start()
            sends[s, d] = copy
        arrived[s, e] = message[s, e]

    base = 14
    halves = (pl.ds(0, 2048), pl.ds(2048, 2048))

    def first_gather(s):
        for d in range(1, 8):
            sends[s, d].wait()
        ordered = jnp.dot(
            gather_perm[...], arrived[s].reshape(128, 512), preferred_element_type=F32
        ).astype(BF16)
        for k in range(8):
            h, at = divmod(k, 4)
            rows[s, h, z, x, :, at * 512 : (at + 1) * 512] = ordered[k * 16 : (k + 1) * 16]
        copies = []
        for h in range(2):
            for d in (1, 2, 3):
                copy = remote(
                    rows.at[s, h, z, x],
                    rows.at[s, h, z, x],
                    sems,
                    base + s * GATHER + h * 3 + d - 1,
                    (dev_x if h == 0 else dev_z)(d),
                )
                copy.start()
                copies.append(copy)
        return copies

    def band(s, h, at, half=None):
        along = pl.ds(0, 4) if half is None else pl.ds(2 * half, 2)
        return rows.at[s, h, at, along] if h == 0 else rows.at[s, h, along, at]

    def second_gather(s, firsts):
        copies = []
        at0 = base + s * GATHER + 6
        for h in range(2):
            for copy in firsts[h * 3 : h * 3 + 3]:
                copy.wait()
            dev, at = (dev_z, z) if h == 0 else (dev_x, x)
            for i, d in enumerate((1, 3)):
                copy = remote(band(s, h, at), band(s, h, at), sems, at0 + h * 4 + i, dev(d))
                copy.start()
                copies.append(copy)
        return copies

    def third_gather(s, seconds):
        copies = []
        at0 = base + s * GATHER + 6
        for h in range(2):
            dev, at = (dev_z, z) if h == 0 else (dev_x, x)
            for i, d in enumerate((1, 3)):
                seconds[h * 2 + i].wait()
                source = lax.rem(at + 4 - d, 4)
                copy = remote(
                    band(s, h, source, i), band(s, h, source, i), sems, at0 + h * 4 + 2 + i, dev(d)
                )
                copy.start()
                copies.append(copy)
        return copies

    def compute(s):
        wide = 256

        def hidden(t, carry):
            at = pl.ds(pl.multiple_of(t * wide, wide), wide)
            g = jnp.zeros((256, wide), F32)
            u = jnp.zeros((256, wide), F32)
            for h in range(2):
                piece = rows[s, h].reshape(256, 2048)
                nt = (((1,), (1,)), ((), ()))
                g = g + lax.dot_general(piece, gate[at, halves[h]], nt, preferred_element_type=F32)
                u = u + lax.dot_general(piece, up[at, halves[h]], nt, preferred_element_type=F32)
            act[:, at] = (g / (1.0 + jnp.exp(-g)) * u).astype(BF16)
            return carry

        lax.fori_loop(0, 512 // wide, hidden, 0)

    def project(s):
        for h in range(2):

            def columns(t, carry, h=h):
                at = pl.ds(pl.multiple_of(t * 512, 512), 512)
                from_ = pl.ds(pl.multiple_of(h * 2048 + t * 512, 512), 512)
                value = jnp.dot(act[...], down[:, from_], preferred_element_type=F32)
                part[s, h, :, :, :, at] = value.astype(BF16).reshape(4, 4, 16, 512)
                return carry

            lax.fori_loop(0, 4, columns, 0)

    base2 = base + 2 * GATHER

    def pband(ref, h, at, half=None):
        along = pl.ds(0, 4) if half is None else pl.ds(2 * half, 2)
        return ref.at[h, at, along] if h == 0 else ref.at[h, along, at]

    def first_reduce(s):
        copies = []
        for h in range(2):
            dev, at = (dev_z, z) if h == 0 else (dev_x, x)
            far = lax.rem(at + 2, 4)
            for i, d in enumerate((1, 3)):
                copy = remote(
                    pband(part.at[s], h, far, i),
                    got_hop.at[s, h, i],
                    sems,
                    base2 + s * GATHER + h * 4 + i,
                    dev(d),
                )
                copy.start()
                copies.append(copy)
        return copies

    def second_reduce(s, firsts):
        copies = []
        for h in range(2):
            dev, at = (dev_z, z) if h == 0 else (dev_x, x)
            for i, d in enumerate((1, 3)):
                firsts[h * 2 + i].wait()
                to = lax.rem(at + d, 4)
                if h == 0:
                    value = part[s, h, to, 2 * i : 2 * i + 2].astype(F32)
                    part[s, h, to, 2 * i : 2 * i + 2] = (
                        value + got_hop[s, h, i].astype(F32)
                    ).astype(BF16)
                else:
                    for j in range(2):
                        value = part[s, h, 2 * i + j, to].astype(F32)
                        part[s, h, 2 * i + j, to] = (
                            value + got_hop[s, h, i, j].astype(F32)
                        ).astype(BF16)
                copy = remote(
                    pband(part.at[s], h, to),
                    got_full.at[s, h, i],
                    sems,
                    base2 + s * GATHER + h * 4 + 2 + i,
                    dev(d),
                )
                copy.start()
                copies.append(copy)
        return copies

    def third_reduce(s, seconds):
        copies = []
        for h in range(2):
            for i in range(2):
                seconds[h * 2 + i].wait()
            for j in range(4):
                kept = part[s, h, z, j] if h == 0 else part[s, h, j, x]
                total = kept.astype(F32)
                for i in range(2):
                    total = total + got_full[s, h, i, j].astype(F32)
                quad[s, h, j] = total.astype(BF16)
            dev, at = (dev_x, x) if h == 0 else (dev_z, z)
            for d in (1, 2, 3):
                copy = remote(
                    quad.at[s, h, lax.rem(at + d, 4)],
                    got_quad.at[s, h, d - 1],
                    sems,
                    base2 + s * GATHER + 8 + h * 3 + d - 1,
                    dev(d),
                )
                copy.start()
                copies.append(copy)
        return copies

    base3 = base2 + 2 * GATHER

    def send_back(s, thirds):
        pieces = []
        for h in range(2):
            for copy in thirds[h * 3 : h * 3 + 3]:
                copy.wait()
            at = x if h == 0 else z
            total = quad[s, h, at].astype(F32)
            for d in range(3):
                total = total + got_quad[s, h, d].astype(F32)
            total = total.astype(BF16)
            pieces.extend(total[:, k * 512 : (k + 1) * 512] for k in range(4))
        stack = jnp.concatenate(pieces, axis=0)
        value = jnp.dot(back_perm[...], stack, preferred_element_type=F32).astype(BF16)
        reply[s] = value.reshape(8, 16, 512)
        copies = []
        for d in range(1, 8):
            copy = remote(
                reply.at[s, lax.rem(e + d, 8)],
                returned.at[s, e],
                sems,
                base3 + s * 7 + d - 1,
                dev_e(d),
            )
            copy.start()
            copies.append(copy)
        returned[s, e] = reply[s, e]
        return copies

    first0 = first_gather(0)
    first1 = first_gather(1)
    second0 = second_gather(0, first0)
    third0 = third_gather(0, second0)
    second1 = second_gather(1, first1)
    for copy in third0:
        copy.wait()
    for load in loads[:2]:
        load.wait()
    compute(0)
    third1 = third_gather(1, second1)
    loads[2].wait()
    project(0)
    hop0 = first_reduce(0)
    for copy in third1:
        copy.wait()
    full0 = second_reduce(0, hop0)
    compute(1)
    project(1)
    hop1 = first_reduce(1)
    quad0 = third_reduce(0, full0)
    full1 = second_reduce(1, hop1)
    back0 = send_back(0, quad0)
    quad1 = third_reduce(1, full1)
    back1 = send_back(1, quad1)
    for copy in back0 + back1:
        copy.wait()
    replies = returned[...].reshape(256, 512)
    value = jnp.dot(mix_high[...], replies, preferred_element_type=F32)
    value = value + jnp.dot(mix_low[...], replies, preferred_element_type=F32)
    for k in range(8):
        cols = slice(k * 512, (k + 1) * 512)
        out[:, cols] = res[:, cols] + value[k * 8 : (k + 1) * 8]


def expert_layer(res, spread, gather_perm, back_perm, mix_high, mix_low, gate, up, down):
    vmem = pl.BlockSpec(memory_space=pltpu.VMEM)
    hbm = pl.BlockSpec(memory_space=pl.ANY)
    count = 14 + 4 * GATHER + 14
    return pl.pallas_call(
        expert_kernel,
        out_shape=jax.ShapeDtypeStruct((8, 4096), F32),
        in_specs=[vmem] * 6 + [hbm] * 3,
        out_specs=vmem,
        scratch_shapes=[
            pltpu.VMEM((512, 4096), BF16),
            pltpu.VMEM((512, 4096), BF16),
            pltpu.VMEM((512, 4096), BF16),
            pltpu.VMEM((2, 8, 16, 512), BF16),
            pltpu.VMEM((2, 8, 16, 512), BF16),
            pltpu.VMEM((2, 2, 4, 4, 16, 2048), BF16),
            pltpu.VMEM((256, 512), BF16),
            pltpu.VMEM((2, 2, 4, 4, 16, 2048), BF16),
            pltpu.VMEM((16, 128), BF16),
            pltpu.VMEM((16, 128), BF16),
            pltpu.VMEM((2, 2, 2, 2, 16, 2048), BF16),
            pltpu.VMEM((2, 2, 2, 4, 16, 2048), BF16),
            pltpu.VMEM((2, 2, 4, 16, 2048), BF16),
            pltpu.VMEM((2, 2, 3, 16, 2048), BF16),
            pltpu.VMEM((2, 8, 16, 512), BF16),
            pltpu.VMEM((2, 8, 16, 512), BF16),
            pltpu.SemaphoreType.DMA((3,)),
            pltpu.SemaphoreType.DMA((count,)),
            pltpu.SemaphoreType.DMA((count,)),
        ],
        compiler_params=pltpu.CompilerParams(
            collective_id=2, has_side_effects=True, vmem_limit_bytes=48 * MIB
        ),
        name="experts",
    )(res, spread, gather_perm, back_perm, mix_high, mix_low, gate, up, down)


def tables(expert_ids, route_weight):
    named = expert_ids[..., None] == jnp.arange(8, dtype=jnp.int32)
    hit = jnp.any(named, axis=2)
    earlier = jnp.arange(4)[:, None] > jnp.arange(4)[None, :]
    slot = jnp.sum((earlier[None, :, :, None] & hit[:, None, :, :]).astype(jnp.int32), axis=2)
    chosen = hit[..., None] & (slot[..., None] == jnp.arange(2))
    weight = jnp.sum(jnp.where(named, route_weight[..., None], 0.0), axis=2)
    same_step = jnp.eye(2, dtype=bool)
    same_chunk = jnp.eye(8, dtype=bool)
    pick = jnp.transpose(chosen, (0, 2, 3, 1))[:, :, None, :, None, None, :]
    mask = (
        pick
        & same_chunk[None, None, :, None, :, None, None]
        & same_step[:, None, None, None, None, :, None]
    )
    weights = jnp.transpose(weight, (0, 2, 1))[:, :, None, None, None, None, :]
    spread = mask.astype(BF16).reshape(256, 64)
    mix = jnp.where(mask, weights, 0.0).reshape(256, 64).T
    high = mix.astype(BF16)
    low = (mix - high.astype(F32)).astype(BF16)
    return spread, high, low


def shards(
    layer_in,
    conv_state,
    ssm_state,
    proj_inner,
    proj_gate,
    conv_weight,
    conv_bias,
    delta_down,
    state_proj,
    delta_up,
    delta_bias,
    decay_log,
    skip_gain,
    proj_out,
    expert_gate,
    expert_up,
    expert_down,
    expert_ids,
    route_weight,
):
    spread, mix_high, mix_low = tables(expert_ids, route_weight)
    index = jnp.arange(128)
    chunk, source, slot = index // 16, index // 2 % 8, index % 2
    gather_perm = ((source * 16 + chunk * 2 + slot)[:, None] == index[None, :]).astype(BF16)
    back_perm = gather_perm.T

    flat = layer_in.reshape(256, 4096)
    flat_float = flat.astype(F32)
    scale = lax.rsqrt(jnp.mean(flat_float * flat_float, axis=-1, keepdims=True) + 1e-06)
    conv_in = (jnp.dot(flat, proj_inner, preferred_element_type=F32) * scale).astype(BF16)
    gate_branch = jnp.dot(flat, proj_gate, preferred_element_type=F32) * scale
    steps = [conv_state[:, 0], conv_state[:, 1], conv_state[:, 2], conv_in[:128], conv_in[128:]]
    floats = [v.astype(F32) for v in steps]
    acts = []
    for s in range(2):
        total = conv_bias[None]
        for k in range(4):
            total = total + floats[s + k] * conv_weight[k][None]
        acts.append(jax.nn.silu(total).astype(BF16))
    activated = jnp.concatenate(acts, axis=0)
    conv_final = jnp.stack(steps[2:], axis=1)
    delta_part = jnp.dot(activated, delta_down, preferred_element_type=F32).astype(BF16)
    state_part = lax.dot_general(
        activated,
        state_proj.reshape(32, 128),
        (((1,), (1,)), ((), ())),
        preferred_element_type=F32,
    ).astype(BF16)
    state_part = jnp.pad(state_part, ((0, 0), (0, 224)))
    both = jnp.stack([delta_part, state_part], axis=0).reshape(2, 2, 32, 4, 256)
    part = jnp.transpose(both, (2, 0, 1, 3, 4)).reshape(32, 16, 256)
    summed = small_sum(part).reshape(32, 2, 2, 4, 256)
    delta_normed = jnp.transpose(summed[:, 0], (1, 0, 2, 3)).reshape(256, 256)
    state_in = jnp.transpose(summed[:, 1, :, :, :64], (1, 0, 2, 3)).reshape(2, 128, 64)
    state_in = state_in[..., :32].astype(F32) + state_in[..., 32:].astype(F32)
    step_size = jax.nn.softplus(
        jnp.dot(delta_normed, delta_up, preferred_element_type=F32) + delta_bias
    ).reshape(2, 128, 128)
    rates = jnp.exp(decay_log)[None]
    act_float = activated.astype(F32).reshape(2, 128, 128)
    gate_branch = gate_branch.reshape(2, 128, 128)
    gated = []
    for s in range(2):
        size = step_size[s][:, None, :]
        ssm_state = (
            jnp.exp(-size * rates) * ssm_state
            + size * state_in[s, :, :16, None] * act_float[s][:, None, :]
        )
        readout = jnp.sum(ssm_state * state_in[s, :, 16:, None], axis=1)
        gated.append(
            ((readout + skip_gain * act_float[s]) * jax.nn.silu(gate_branch[s])).astype(BF16)
        )
    gated = jnp.stack(gated).reshape(2, 4, 2, 4, 4, 128)
    gated = jnp.transpose(gated, (1, 3, 2, 0, 4, 5)).reshape(256, 128)
    place_ = lax.axis_index(("expert", "tensor"))
    own = lax.dynamic_slice_in_dim(layer_in, place_ * 4, 4, 1).reshape(8, 4096)
    residual = mixer_out(gated, proj_out, own)
    out = expert_layer(
        residual, spread, gather_perm, back_perm, mix_high, mix_low,
        expert_gate, expert_up, expert_down,
    )
    layer_out = out.astype(BF16).reshape(2, 4, 4096)
    return (layer_out, conv_final, ssm_state)


def solution(mesh):
    channels = ("expert", "tensor")
    rows = ("dp", "expert", "tensor")
    placed = (
        P(None, "dp", None),
        P("dp", None, channels),
        P("dp", None, channels),
        P(None, channels),
        P(None, channels),
        P(None, channels),
        P(channels),
        P(channels, None),
        P(None, None, channels),
        P(None, channels),
        P(channels),
        P(None, channels),
        P(channels),
        P(channels, None),
        P("expert", ("dp", "tensor"), None),
        P("expert", ("dp", "tensor"), None),
        P("expert", ("dp", "tensor"), None),
        P(None, rows, None),
        P(None, rows, None),
    )
    return jax.shard_map(
        shards,
        mesh=mesh,
        in_specs=placed,
        out_specs=(P(None, rows, None), P("dp", None, channels), P("dp", None, channels)),
        check_vma=False,
    )
```

time: 436 us -> 134 us (0.31)
  waiting for transfers between devices: 178 us -> 0 us
  blocking collectives: 125 us -> 0 us
  Pallas kernels: 0 us -> 110 us
  matrix products: 46.3 us -> 1.92 us
  starting transfers between devices: 20.8 us -> 0 us
  other arithmetic: 24.6 us -> 9.45 us
  local copies, waits for them, and re-layouts: 25.4 us -> 11.4 us
  between operations: 15.1 us -> 1.15 us
    psum x1 -> x0, blocking collectives: 125 us -> none  [mixer_step(): lax.psum(state_part.astype(jnp.bfloat16), ('expert', 'tensor'))]
    pallas_call x0 -> x3, Pallas kernels: none -> 110 us  [the longest x1 70.3 us: expert_layer(): pl.pallas_call(expert_kernel, out_shape=jax.ShapeDtypeStruct((8, 4096), F...]
    unnamed x3 -> x0, waiting for transfers between devices: 105 us -> none
    all_to_all x4 -> x0, waiting for transfers between devices: 73.6 us -> none  [the longest x2 39 us: expert_layer(): lax.all_to_all(copies, ('dp', 'expert', 'tensor'), split_axis=0, concat_a...]
    dot_general x18 -> x5, matrix products: 46.3 us -> 1.92 us  [the longest x1 0.71 us: shards(): jnp.dot(flat, proj_inner, preferred_element_type=F32) * scale]
    all_to_all x4 -> x0, starting transfers between devices: 20.7 us -> none  [the longest x2 13 us: expert_layer(): lax.all_to_all(copies, ('dp', 'expert', 'tensor'), split_axis=0, concat_a...]
    reduce_sum x12 -> x4, other arithmetic: 17.1 us -> 4.88 us  [the longest x1 2.47 us: shards(): readout = jnp.sum(ssm_state * state_in[s, :, 16:, None], axis=1)]
    convert_element_type x4 -> x1, local copies, waits for them, and re-layouts: 10.4 us -> 1.06 us  [tables(): spread = mask.astype(BF16).reshape(256, 64)]
  transfers between devices with their start and end apart: 6 -> 0, of which waited for: 5 -> 0; matrix products, arithmetic and copies ran while one was open for 13% -> 0% of each run, Pallas kernels for 0% -> 0%
where the time goes in v1:
time: 134 us
  Pallas kernels  110 us (82%)
  local copies, waits for them, and re-layouts  11.4 us (9%)
  other arithmetic  9.45 us (7%)
  matrix products  1.92 us (1%)
    pallas_call x1, Pallas kernels, expert_layer(): pl.pallas_call(expert_kernel, out_shape=jax.ShapeDtypeStruct((8, 4096), F...  70.3 us
    pallas_call x1, Pallas kernels, small_sum(): pl.pallas_call(small_sum_kernel, out_shape=jax.ShapeDtypeStruct((32, 16,...  20.6 us
    pallas_call x1, Pallas kernels, mixer_out(): pl.pallas_call(mixer_out_kernel, out_shape=jax.ShapeDtypeStruct((8, 4096)...  18.9 us
    select_n x2, local copies, waits for them, and re-layouts, tables(): mix = jnp.where(mask, weights, 0.0).reshape(256, 64).T  4.61 us
    unnamed x42, local copies, waits for them, and re-layouts  3.27 us

profile of v1, /device:TPU:1, one launch (start us, length us, event | category | flops | bytes accessed | tf_op | source)
XLA Modules:
  0.0 133.7 jit_solution(3722499192080030578)
XLA Ops:
  0.6 0.0 copy-start
  0.6 0.0 copy-start.3
  0.7 2.2 %multiply_reduce_fusion = f32[2,128]{1,0:T(2,128)S(1)} fusion(bf16[2,128,4096]{2,1,0:T(8,128)(2,1)} %param.19), kind=kLoop, calls=%fused_computation.2 | loop fusion | flops 3145472 | bytes 2098176 | tf_op jit(solution)/shard_map/reduce_sum | solution.py:594
  2.9 0.0 copy-start.9
  2.9 0.0 copy-start.15
  2.9 0.0 copy-start.18
  3.0 0.2 copy-done.3
  3.2 0.7 fusion
  3.9 0.0 copy-start.7
  3.9 0.6 copy-done.7
  4.6 0.1 multiply_convert_fusion.3
  4.7 0.1 convolution_convert_fusion.1
  4.8 0.1 copy.53
  5.0 0.2 convolution_convert_fusion
  5.2 0.2 maximum_bitcast_fusion
  5.4 0.1 copy.41
  5.5 0.1 reshape.203.part
  5.6 0.0 copy-start.11
  5.6 0.0 copy-start.6
  5.6 20.6 %small_sum.1 = bf16[32,16,256]{2,1,0:T(8,128)(2,1)S(1)} custom-call(bf16[32,16,256]{2,1,0:T(8,128)(2,1)S(1)} %reshape.203.part), custom_call_target="tpu_custom_call" | custom-call | tf_op jit(solution)/shard_map/small_sum/pallas_call | solution.py:102
  26.2 0.1 reshape.204
  26.4 0.2 compare_select_fusion
  26.7 0.0 copy-start.5
  26.7 0.1 convert_add_fusion
  26.8 0.1 slice_bitcast_fusion.2
  27.0 2.5 %multiply_reduce_fusion.1 = (f32[128,128]{1,0:T(8,128)S(1)}, f32[128,16,128]{2,1,0:T(8,128)}, f32[128,128]{1,0:T(8,128)S(1)}) fusion(f32[128,16]{1,0:T(8,128)S(1)} %get-tuple-element.13, f32[128,128]{1,0:T(8,128)S(1)} %get-tuple-element.30, f32[128,16]{1,0:T(8,128)S(1)} %get-tuple-element.14, f32[128,128]{1,0:T(8,128)S(1)} %get-tuple-element.18, ...), kind=kLoop, calls=%fused_computation.9 | loop fusion | flops 3637248 | bytes 2662400 | tf_op jit(solution)/shard_map/reduce_sum | solution.py:634
  29.4 0.0 copy-start.12
  29.5 0.7 convolution_multiply_fusion
  30.2 0.1 multiply_convert_fusion.1
  30.3 0.9 constant_dynamic-slice_fusion
  31.3 18.9 %mixer_out.1.res = f32[8,4096]{1,0:T(8,128)S(1)} custom-call(bf16[256,128]{1,0:T(8,128)(2,1)S(1)} %bitcast.68, bf16[128,4096]{1,0:T(8,128)(2,1)S(1)} %copy-done.2, bf16[8,4096]{1,0:T(8,128)(2,1)S(1)} %reshape.208.own), custom_call_target="tpu_custom_call" | custom-call | tf_op jit(solution)/shard_map/mixer_out/pallas_call | solution.py:203
  50.2 0.1 fusion.13
  50.3 0.1 convert_reduce_fusion
  50.4 0.1 copy.47
  50.5 0.1 copy.46
  50.6 0.2 broadcast_and_fusion
  50.9 0.1 select_reduce_fusion
  51.0 0.1 copy.48
  51.0 1.6 %and_select_fusion = f32[2,8,8,2,8,2,4]{6,5,4,3,2,1,0:T(2,128)S(1)} fusion(pred[2,2]{1,0:T(4,128)(4,1)S(1)} %iota_compare_fusion.5, pred[2,8,8,2,8,4]{5,4,3,2,1,0:T(8,128)(4,1)S(1)} %broadcast_and_fusion, f32[2,8,4]{2,1,0:T(8,128)S(1)} %copy.48), kind=kLoop, calls=%fused_computation | loop fusion | flops 32768 | bytes 73988 | tf_op jit(solution)/shard_map/jit(_where)/select_n | solution.py:559
  52.6 3.6 %select_n.70 = f32[256,64]{1,0:T(8,128)} reshape(f32[2,8,8,2,8,2,4]{6,5,4,3,2,1,0:T(2,128)S(1)} %and_select_fusion) | data formatting | bytes 131072 | tf_op jit(solution)/shard_map/jit(_where)/select_n | solution.py:559
  56.2 1.0 copy.49
  57.2 1.4 %and_convert_fusion = bf16[2,8,8,2,8,2,4]{6,5,4,3,2,1,0:T(2,128)(2,1)S(1)} fusion(pred[2,2]{1,0:T(4,128)(4,1)S(1)} %iota_compare_fusion.5, pred[2,8,8,2,8,4]{5,4,3,2,1,0:T(8,128)(4,1)S(1)} %broadcast_and_fusion), kind=kLoop, calls=%fused_computation.1 | loop fusion | flops 32768 | bytes 40964 | tf_op jit(solution)/shard_map/convert_element_type | solution.py:558
  58.7 1.1 reshape.213.spread
  59.7 0.1 fusion.11
  59.8 2.2 %copy-done.1 = bf16[1,512,4096]{2,1,0:T(8,128)(2,1)S(1)} copy-done((bf16[1,512,4096]{2,1,0:T(8,128)(2,1)S(1)}, bf16[1,512,4096]{2,1,0:T(8,128)(2,1)}, u32[]{:S(2)}) %copy-start.1) | copy-done | bytes 4194328
  62.0 70.3 %experts.1 = f32[8,4096]{1,0:T(8,128)S(1)} custom-call(f32[8,4096]{1,0:T(8,128)S(1)} %mixer_out.1.res, bf16[256,64]{1,0:T(8,128)(2,1)S(1)} %reshape.213.spread, bf16[128,128]{1,0:T(8,128)(2,1)S(1)} %get-tuple-element.29.gather_perm, bf16[128,128]{1,0:T(8,128)(2,1)S(1)} %get-tuple-element.28.back_perm, bf16[64,256]{1,0:T(8,128)(2,1)S(1)} %get-tuple-element.4.mix_high, ...), custom_call_target="tpu_custom_call" | custom-call | tf_op jit(solution)/shard_map/experts/pallas_call | solution.py:509
  132.3 0.7 reshape.209
  133.0 0.7 pad_maximum_fusion
  (52 shorter events, 0.5 us)
Async XLA Ops:
  0.6 2.3 %copy-start = (bf16[4096,128]{1,0:T(8,128)(2,1)S(1)}, bf16[4096,128]{1,0:T(8,128)(2,1)}, u32[]{:S(2)}) copy-start(bf16[4096,128]{1,0:T(8,128)(2,1)} %param.22) | copy-start | bytes 3145732
  0.6 2.5 %copy-start.3 = (bf16[2,128,4096]{2,1,0:T(8,128)(2,1)S(1)}, bf16[2,128,4096]{2,1,0:T(8,128)(2,1)}, u32[]{:S(2)}) copy-start(bf16[2,128,4096]{2,1,0:T(8,128)(2,1)} %param.19) | copy-start | bytes 6291460
  2.9 1.0 copy-start.13
  2.9 1.6 %copy-start.9 = (bf16[128,3,128]{2,0,1:T(8,128)(2,1)S(1)}, bf16[128,3,128]{2,0,1:T(8,128)(2,1)}, u32[]{:S(2)}) copy-start(bf16[128,3,128]{2,0,1:T(8,128)(2,1)} %param.20) | copy-start | bytes 294916
  2.9 1.6 %copy-start.15 = (f32[128]{0:T(128)S(1)}, f32[128]{0:T(128)}, u32[]{:S(2)}) copy-start(f32[128]{0:T(128)} %param.25) | copy-start | bytes 1540
  2.9 1.7 %copy-start.18 = (bf16[2,16,128]{2,1,0:T(8,128)(2,1)S(1)}, bf16[2,16,128]{2,1,0:T(8,128)(2,1)}, u32[]{:S(2)}) copy-start(bf16[2,16,128]{2,1,0:T(8,128)(2,1)} %param.27) | copy-start | bytes 24580
  2.9 2.1 %copy-start.10 = (bf16[128,256]{1,0:T(8,128)(2,1)S(1)}, bf16[128,256]{1,0:T(8,128)(2,1)}, u32[]{:S(2)}) copy-start(bf16[128,256]{1,0:T(8,128)(2,1)} %param.26) | copy-start | bytes 196612
  3.9 0.6 copy-start.7
  4.8 21.6 %copy-start.17 = (bf16[256,128]{1,0:T(8,128)(2,1)S(1)}, bf16[256,128]{1,0:T(8,128)(2,1)}, u32[]{:S(2)}) copy-start(bf16[256,128]{1,0:T(8,128)(2,1)} %param.28) | copy-start | bytes 196612
  4.8 21.6 %copy-start.19 = (f32[128]{0:T(128)S(1)}, f32[128]{0:T(128)}, u32[]{:S(2)}) copy-start(f32[128]{0:T(128)} %param.29) | copy-start | bytes 1540
  5.6 21.3 %copy-start.11 = (f32[16,128]{1,0:T(8,128)S(1)}, f32[16,128]{1,0:T(8,128)}, u32[]{:S(2)}) copy-start(f32[16,128]{1,0:T(8,128)} %param.30) | copy-start | bytes 24580
  5.6 21.4 %copy-start.6 = (f32[128,16,128]{2,1,0:T(8,128)S(1)}, f32[128,16,128]{2,1,0:T(8,128)}, u32[]{:S(2)}) copy-start(f32[128,16,128]{2,1,0:T(8,128)} %param.21) | copy-start | bytes 3145732
  26.6 2.8 %copy-start.4 = (bf16[2,128,4096]{2,1,0:T(8,128)(2,1)S(1)}, bf16[2,128,4096]{2,1,0:T(8,128)(2,1)}, u32[]{:S(2)}) copy-start(bf16[2,128,4096]{2,1,0:T(8,128)(2,1)} %param.19) | copy-start | bytes 6291460
  26.7 2.8 %copy-start.5 = (bf16[4096,128]{1,0:T(8,128)(2,1)S(1)}, bf16[4096,128]{1,0:T(8,128)(2,1)}, u32[]{:S(2)}) copy-start(bf16[4096,128]{1,0:T(8,128)(2,1)} %param.23) | copy-start | bytes 3145732
  29.4 0.7 copy-start.16
  29.4 1.9 %copy-start.2 = (bf16[128,4096]{1,0:T(8,128)(2,1)S(1)}, bf16[128,4096]{1,0:T(8,128)(2,1)}, u32[]{:S(2)}) copy-start(bf16[128,4096]{1,0:T(8,128)(2,1)} %weight.1) | copy-start | bytes 3145732
  29.4 20.8 %copy-start.12 = (s32[2,4,2]{1,2,0:T(2,128)S(1)}, s32[2,4,2]{1,2,0:T(2,128)}, u32[]{:S(2)}) copy-start(s32[2,4,2]{1,2,0:T(2,128)} %param.36) | copy-start | bytes 196
  30.2 20.7 %copy-start.14 = (f32[2,4,2]{1,2,0:T(2,128)S(1)}, f32[2,4,2]{1,2,0:T(2,128)}, u32[]{:S(2)}) copy-start(f32[2,4,2]{1,2,0:T(2,128)} %param.37) | copy-start | bytes 196
  59.8 2.2 %copy-start.1 = (bf16[1,512,4096]{2,1,0:T(8,128)(2,1)S(1)}, bf16[1,512,4096]{2,1,0:T(8,128)(2,1)}, u32[]{:S(2)}) copy-start(bf16[1,512,4096]{2,1,0:T(8,128)(2,1)} %gate_hbm.1) | copy-start | bytes 12582916
  62.0 71.0 %copy-start.8 = (bf16[256,128]{1,0:T(8,128)(2,1)S(1)}, bf16[256,128]{1,0:T(8,128)(2,1)}, u32[]{:S(2)}) copy-start(bf16[256,128]{1,0:T(8,128)(2,1)} %copy-done.7) | copy-start | bytes 196612
  62.0 71.0 %slice-start = ((bf16[128,3,128]{2,0,1:T(8,128)(2,1)}), bf16[128,1,128]{2,0,1:T(8,128)(2,1)S(1)}, s32[]{:S(2)}) async-start(bf16[128,3,128]{2,0,1:T(8,128)(2,1)} %param.20), calls=%async_computation | async-start | bytes 65536 | tf_op jit(solution)/shard_map/slice | solution.py:597

commit v2 on v1

v2 whole, which is shorter than its diff:
```python
import functools

import jax
import jax.numpy as jnp
from jax import lax
from jax.experimental import pallas as pl
from jax.experimental.pallas import tpu as pltpu
from jax.sharding import PartitionSpec as P

MESH = pl.DeviceIdType.MESH
F32 = jnp.float32
BF16 = jnp.bfloat16
MIB = 2**20


def place():
    z, e, x = lax.axis_index("dp"), lax.axis_index("expert"), lax.axis_index("tensor")
    return z, lax.div(e, 2), lax.rem(e, 2), x


def remote(src, dst, sems, at, device):
    return pltpu.make_async_remote_copy(
        src_ref=src,
        dst_ref=dst,
        send_sem=sems[0].at[at],
        recv_sem=sems[1].at[at],
        device_id=device,
        device_id_type=MESH,
    )


def greet(devices):
    barrier = pltpu.get_barrier_semaphore()
    for device in devices:
        pl.semaphore_signal(barrier, inc=1, device_id=device, device_id_type=MESH)
    pl.semaphore_wait(barrier, len(devices))


def silu(v):
    return v / (1.0 + jnp.exp(-v))


PIECES = 4


def mixer_in_kernel(
    rows_hbm, inner_hbm, gate_hbm, conv_state, conv_weight, conv_bias, delta_down, state_proj,
    delta_up, delta_bias,
    conv_out, act_out, gate_out, size_out, state_out,
    rows, inner, gate, local, part, got, both, recv, out, one, other, send_a, recv_a, send_b, recv_b,
):
    z, y, c, x = place()
    me = y * 4 + x
    width = 4096 // PIECES
    loads = []
    for k in range(PIECES):
        cut = pl.ds(k * width, width)
        three = []
        for i, (a, b) in enumerate(
            (
                (rows_hbm.at[:, cut], rows.at[:, cut]),
                (inner_hbm.at[cut], inner.at[cut]),
                (gate_hbm.at[cut], gate.at[cut]),
            )
        ):
            load = pltpu.make_async_copy(a, b, local.at[k * 3 + i])
            load.start()
            three.append(load)
        loads.append(three)

    def chip(p):
        return (z, lax.div(p, 4) * 2 + c, lax.rem(p, 4))

    sibling = (z, y * 2 + 1 - c, x)
    barrier = pltpu.get_barrier_semaphore()
    pl.semaphore_signal(barrier, inc=1, device_id=sibling, device_id_type=MESH)

    def signal(i, carry):
        pl.semaphore_signal(
            barrier, inc=1, device_id=chip(lax.rem(me + i, 16)), device_id_type=MESH
        )
        return carry

    lax.fori_loop(1, 16, signal, 0)

    squares = jnp.zeros((256, 1), F32)
    conv_in = jnp.zeros((256, 128), F32)
    for k in range(PIECES):
        loads[k][0].wait()
        loads[k][1].wait()
        piece = rows[:, k * width : (k + 1) * width]
        conv_in = conv_in + jnp.dot(
            piece, inner[k * width : (k + 1) * width], preferred_element_type=F32
        )
        wide = piece.astype(F32)
        squares = squares + jnp.sum(wide * wide, axis=1, keepdims=True)
    scale = lax.rsqrt(squares * (1.0 / 4096) + 1e-06)
    conv_in = (conv_in * scale).astype(BF16)
    conv_out[...] = conv_in
    conv_in = conv_in.astype(F32)
    window = [conv_state[k].astype(F32) for k in range(3)] + [conv_in[:128], conv_in[128:]]
    acts = []
    for s in range(2):
        total = conv_bias[...]
        for k in range(4):
            total = total + window[s + k] * conv_weight[k : k + 1]
        acts.append(silu(total))
    activated = jnp.concatenate(acts, axis=0).astype(BF16)
    act_out[...] = activated
    delta = jnp.dot(activated, delta_down[...], preferred_element_type=F32)
    state = lax.dot_general(
        activated, state_proj[...], (((1,), (1,)), ((), ())), preferred_element_type=F32
    )
    state = jnp.concatenate([state, jnp.zeros((256, 224), F32)], axis=1)
    blocks = jnp.concatenate([delta.reshape(32, 8, 256), state.reshape(32, 8, 256)], axis=1)
    part[...] = blocks.astype(BF16).reshape(2, 16, 16, 256)

    pl.semaphore_wait(barrier, 16)
    swap = remote(part.at[1 - c], got, (one, other), 0, sibling)
    swap.start()
    swap.wait()
    both[...] = (part[c].astype(F32) + got[...].astype(F32)).astype(BF16)

    def first(i):
        p = lax.rem(me + i, 16)
        return remote(both.at[p], recv.at[i - 1], (send_a, recv_a), i - 1, chip(p))

    def start_first(i, carry):
        first(i).start()
        return carry

    lax.fori_loop(1, 16, start_first, 0)

    gated = jnp.zeros((256, 128), F32)
    for k in range(PIECES):
        loads[k][2].wait()
        gated = gated + jnp.dot(
            rows[:, k * width : (k + 1) * width],
            gate[k * width : (k + 1) * width],
            preferred_element_type=F32,
        )
    gate_out[...] = silu(gated * scale)

    def add(i, total):
        first(i).wait()
        return total + recv[i - 1].astype(F32)

    total = lax.fori_loop(1, 16, add, both[me].astype(F32))
    low, state = total[:8], total[8:]
    normed = low * lax.rsqrt(jnp.mean(low * low, axis=-1, keepdims=True) + 1e-06)
    high = state.astype(BF16).astype(F32)
    rest = state - high
    split = jnp.concatenate([high[:, :32], rest[:, :32], state[:, 64:]], axis=1)
    out[c, me] = jnp.concatenate([normed, split], axis=0).astype(BF16)

    def second(i):
        return remote(
            out.at[c, me], out.at[c, me], (send_b, recv_b), i - 1, chip(lax.rem(me + i, 16))
        )

    def second_from(i):
        p = lax.rem(me + 16 - i, 16)
        return remote(out.at[c, p], out.at[c, p], (send_b, recv_b), i - 1, chip(p))

    def start_second(i, carry):
        second(i).start()
        return carry

    lax.fori_loop(1, 16, start_second, 0)

    def wait_second(i, carry):
        second(i).wait_send()
        second_from(i).wait_recv()
        return carry

    lax.fori_loop(1, 16, wait_second, 0)
    swap = remote(out.at[c], out.at[c], (one, other), 1, sibling)
    swap.start()
    swap.wait_send()
    remote(out.at[1 - c], out.at[1 - c], (one, other), 1, sibling).wait_recv()
    summed = out[...].reshape(32, 16, 256).astype(F32)
    normed = summed[:, :8].reshape(256, 256).astype(BF16)
    value = jnp.dot(normed, delta_up[...], preferred_element_type=F32) + delta_bias[...]
    size_out[...] = jnp.maximum(value, 0.0) + jnp.log1p(jnp.exp(-jnp.abs(value)))
    state = summed[:, 8:].reshape(256, 256)
    state_out[...] = state[:, :32] + state[:, 32:64]


def mixer_in(rows, inner, gate, *rest):
    vmem = pl.BlockSpec(memory_space=pltpu.VMEM)
    hbm = pl.BlockSpec(memory_space=pl.ANY)
    return pl.pallas_call(
        mixer_in_kernel,
        out_shape=(
            jax.ShapeDtypeStruct((256, 128), BF16),
            jax.ShapeDtypeStruct((256, 128), BF16),
            jax.ShapeDtypeStruct((256, 128), F32),
            jax.ShapeDtypeStruct((256, 128), F32),
            jax.ShapeDtypeStruct((256, 32), F32),
        ),
        in_specs=[hbm] * 3 + [vmem] * len(rest),
        out_specs=(vmem,) * 5,
        scratch_shapes=[
            pltpu.VMEM((256, 4096), BF16),
            pltpu.VMEM((4096, 128), BF16),
            pltpu.VMEM((4096, 128), BF16),
            pltpu.SemaphoreType.DMA((3 * PIECES,)),
            pltpu.VMEM((2, 16, 16, 256), BF16),
            pltpu.VMEM((16, 16, 256), BF16),
            pltpu.VMEM((16, 16, 256), BF16),
            pltpu.VMEM((15, 16, 256), BF16),
            pltpu.VMEM((2, 16, 16, 256), BF16),
            pltpu.SemaphoreType.DMA((2,)),
            pltpu.SemaphoreType.DMA((2,)),
            pltpu.SemaphoreType.DMA((15,)),
            pltpu.SemaphoreType.DMA((15,)),
            pltpu.SemaphoreType.DMA((15,)),
            pltpu.SemaphoreType.DMA((15,)),
        ],
        compiler_params=pltpu.CompilerParams(
            collective_id=0, has_side_effects=True, vmem_limit_bytes=56 * MIB
        ),
        name="mixer_in",
    )(rows, inner, gate, *rest)


def tables(ids, route, core):
    lane = lax.broadcasted_iota(jnp.int32, (8, 128), 1)
    named = [lane == ids[:, j : j + 1] for j in range(2)]
    hit = (named[0] | named[1]).astype(F32)
    row, col = (lax.broadcasted_iota(jnp.int32, (8, 8), d) for d in range(2))
    earlier = ((col < row) & (col // 4 == row // 4)).astype(F32)
    count = jnp.dot(earlier, hit, preferred_element_type=F32)
    here = lax.broadcasted_iota(jnp.int32, (8, 1), 0) // 4 == core
    at = lax.broadcasted_iota(jnp.int32, (64, 128), 1)
    pick, mix = None, None
    for j in range(2):
        slot = jnp.sum(jnp.where(named[j], count, 0.0), axis=1, keepdims=True).astype(jnp.int32)
        target = jnp.where(here, ids[:, j : j + 1] * 16 + slot, -64)
        mask = at == jnp.concatenate([target + 2 * k for k in range(8)], axis=0)
        weight = jnp.concatenate([route[:, j : j + 1]] * 8, axis=0)
        one = jnp.where(mask, 1.0, 0.0)
        pick = one if j == 0 else pick + one
        mix = one * weight if j == 0 else mix + one * weight
    return pick.astype(BF16), mix


def swap_fields():
    row, col = (lax.broadcasted_iota(jnp.int32, (128, 128), d) for d in range(2))
    swapped = (row // 2 % 8) * 16 + (row // 16) * 2 + row % 2
    return jnp.where(col == swapped, 1.0, 0.0).astype(BF16)


GATHER = 14


def expert_kernel(
    gated, weight, ids, route, layer_hbm, gate_hbm, up_hbm, down_hbm,
    out,
    own, left, first, mine, got0, sums, got1, mid, got2, last, got3, residual,
    gate, up, down, message, arrived, rows, act, part, got_hop, got_full, quad, got_quad,
    reply, returned, local, ss, rs, mss, mrs,
):
    z, y, c, x = place()
    e = y * 2 + c
    sems = (ss, rs)
    mixer_sems = (mss, mrs)
    loads = []
    for i, (a, b) in enumerate(((gate_hbm, gate), (up_hbm, up), (down_hbm, down))):
        load = pltpu.make_async_copy(a.at[0], b, local.at[i])
        load.start()
        loads.append(load)
    chip_rows = pltpu.make_async_copy(
        layer_hbm.at[:, pl.ds(pl.multiple_of(y * 32, 32), 32)], own, local.at[3]
    )
    chip_rows.start()

    def dev_e(d):
        return (z, lax.rem(e + d, 8), x)

    def dev_x(d):
        return (z, e, lax.rem(x + d, 4))

    def dev_y(d):
        return (z, lax.rem(y + d, 4) * 2 + c, x)

    def dev_z(d):
        return (lax.rem(z + d, 4), e, x)

    sibling = (z, y * 2 + 1 - c, x)
    friends = [dev_e(d) for d in range(1, 8)] + [f(d) for f in (dev_x, dev_z) for d in (1, 2, 3)]
    barrier = pltpu.get_barrier_semaphore()
    for friend in friends:
        pl.semaphore_signal(barrier, inc=1, device_id=friend, device_id_type=MESH)

    MIXER = 15
    other = 1 - c

    def product(s, half, q):
        cols = pl.ds(pl.multiple_of(half * 2048 + q * 1024, 1024), 1024)
        return jnp.dot(left[s], weight[:, cols], preferred_element_type=F32)

    def mixer_swap(s):
        copies = []
        for q in range(2):
            copy = remote(first.at[s, q], got0.at[s, q], mixer_sems, s * MIXER + q, sibling)
            copy.start()
            copies.append(copy)
        return copies

    def mixer_first(s, swaps):
        copies = []
        for q in range(2):
            swaps[q].wait()
            both = (mine[s, q] + got0[s, q].astype(F32)).reshape(4, 4, 8, 1024)
            both = jnp.concatenate([both[..., :512], both[..., 512:]], axis=2).astype(BF16)
            if q == 0:
                for at in range(4):
                    for to in range(4):
                        sums[s, q, to, at] = both[at, to]
            else:
                sums[s, q] = both
            dev, at = (dev_x, x) if q == 0 else (dev_y, y)
            for d in (1, 2, 3):
                copy = remote(
                    sums.at[s, q, lax.rem(at + d, 4)],
                    got1.at[s, q, d - 1],
                    mixer_sems,
                    s * MIXER + 2 + q * 3 + d - 1,
                    dev(d),
                )
                copy.start()
                copies.append(copy)
        return copies

    def mixer_second(s, ones):
        copies = []
        for q in range(2):
            for copy in ones[q * 3 : q * 3 + 3]:
                copy.wait()
            total = sums[s, q, x if q == 0 else y].astype(F32)
            for d in range(3):
                total = total + got1[s, q, d].astype(F32)
            mid[s, q] = total.astype(BF16)
            dev, at = (dev_y, y) if q == 0 else (dev_x, x)
            for d in (1, 2, 3):
                copy = remote(
                    mid.at[s, q, lax.rem(at + d, 4)],
                    got2.at[s, q, d - 1],
                    mixer_sems,
                    s * MIXER + 8 + q * 3 + d - 1,
                    dev(d),
                )
                copy.start()
                copies.append(copy)
        return copies

    def mixer_third(s, twos):
        for q in range(2):
            for copy in twos[q * 3 : q * 3 + 3]:
                copy.wait()
            total = mid[s, q, y if q == 0 else x].astype(F32)
            for d in range(3):
                total = total + got2[s, q, d].astype(F32)
            last[s, q] = total
        copy = remote(last.at[s], got3.at[s], mixer_sems, s * MIXER + 14, sibling)
        copy.start()
        return copy

    picks, mixes = [], []
    for s in range(2):
        pick, mix = tables(
            jnp.concatenate([ids[s]] * 2, axis=0), jnp.concatenate([route[s]] * 2, axis=0), c
        )
        picks.append(pick)
        mixes.append(mix)
    swap = swap_fields()

    sends = {}

    row, col = (lax.broadcasted_iota(jnp.int32, (16, 32), d) for d in range(2))
    chosen = jnp.where(col == row // 4 * 16 + x * 4 + row % 4, 1.0, 0.0).astype(BF16)

    def rows_out(s, copy):
        if s == 0:
            chip_rows.wait()
        for half, source in ((c, last), (other, got3)):
            if source is got3:
                copy.wait()
            for q in range(2):
                for k in range(2):
                    cols = pl.ds(pl.multiple_of(half * 2048 + q * 1024 + k * 512, 512), 512)
                    step_rows = jnp.dot(chosen, own[s, :, cols], preferred_element_type=F32)
                    residual[s, :, cols] = source[s, q, k * 8 : k * 8 + 8] + step_rows[:8]
        value = residual[s]
        normed = value * lax.rsqrt(jnp.mean(value * value, axis=-1, keepdims=True) + 1e-06)
        stacked = jnp.concatenate([normed[:, k * 512 : (k + 1) * 512] for k in range(8)], axis=0)
        spread_rows = lax.dot_general(
            picks[s], stacked.astype(BF16), (((0,), (0,)), ((), ())), preferred_element_type=F32
        )
        message[s] = spread_rows.astype(BF16).reshape(8, 16, 512)
        for d in range(1, 8):
            copy = remote(
                message.at[s, lax.rem(e + d, 8)],
                arrived.at[s, e],
                sems,
                s * 7 + d - 1,
                dev_e(d),
            )
            copy.start()
            sends[s, d] = copy
        arrived[s, e] = message[s, e]

    base = 14
    halves = (pl.ds(0, 2048), pl.ds(2048, 2048))

    def first_gather(s):
        for d in range(1, 8):
            sends[s, d].wait()
        ordered = jnp.dot(
            swap, arrived[s].reshape(128, 512), preferred_element_type=F32
        ).astype(BF16)
        for k in range(8):
            h, at = divmod(k, 4)
            rows[s, h, z, x, :, at * 512 : (at + 1) * 512] = ordered[k * 16 : (k + 1) * 16]
        copies = []
        for h in range(2):
            for d in (1, 2, 3):
                copy = remote(
                    rows.at[s, h, z, x],
                    rows.at[s, h, z, x],
                    sems,
                    base + s * GATHER + h * 3 + d - 1,
                    (dev_x if h == 0 else dev_z)(d),
                )
                copy.start()
                copies.append(copy)
        return copies

    def band(s, h, at, half=None):
        along = pl.ds(0, 4) if half is None else pl.ds(2 * half, 2)
        return rows.at[s, h, at, along] if h == 0 else rows.at[s, h, along, at]

    def second_gather(s, firsts):
        copies = []
        at0 = base + s * GATHER + 6
        for h in range(2):
            for copy in firsts[h * 3 : h * 3 + 3]:
                copy.wait()
            dev, at = (dev_z, z) if h == 0 else (dev_x, x)
            for i, d in enumerate((1, 3)):
                copy = remote(band(s, h, at), band(s, h, at), sems, at0 + h * 4 + i, dev(d))
                copy.start()
                copies.append(copy)
        return copies

    def third_gather(s, seconds):
        copies = []
        at0 = base + s * GATHER + 6
        for h in range(2):
            dev, at = (dev_z, z) if h == 0 else (dev_x, x)
            for i, d in enumerate((1, 3)):
                seconds[h * 2 + i].wait()
                source = lax.rem(at + 4 - d, 4)
                copy = remote(
                    band(s, h, source, i), band(s, h, source, i), sems, at0 + h * 4 + 2 + i, dev(d)
                )
                copy.start()
                copies.append(copy)
        return copies

    def compute(s):
        wide = 256

        def hidden(t, carry):
            at = pl.ds(pl.multiple_of(t * wide, wide), wide)
            g = jnp.zeros((256, wide), F32)
            u = jnp.zeros((256, wide), F32)
            for h in range(2):
                piece = rows[s, h].reshape(256, 2048)
                nt = (((1,), (1,)), ((), ()))
                g = g + lax.dot_general(piece, gate[at, halves[h]], nt, preferred_element_type=F32)
                u = u + lax.dot_general(piece, up[at, halves[h]], nt, preferred_element_type=F32)
            act[:, at] = (g / (1.0 + jnp.exp(-g)) * u).astype(BF16)
            return carry

        lax.fori_loop(0, 512 // wide, hidden, 0)

    def project(s, q):
        for h in range(2):
            from_ = slice(h * 2048 + q * 1024, h * 2048 + (q + 1) * 1024)
            value = jnp.dot(act[...], down[:, from_], preferred_element_type=F32)
            part[s, h, q] = value.astype(BF16).reshape(4, 4, 16, 1024)

    base2 = base + 2 * GATHER

    def pband(s, h, q, at, half=None):
        along = pl.ds(0, 4) if half is None else pl.ds(2 * half, 2)
        return part.at[s, h, q, at, along] if h == 0 else part.at[s, h, q, along, at]

    def first_reduce(s, q):
        copies = []
        for h in range(2):
            dev, at = (dev_z, z) if h == 0 else (dev_x, x)
            far = lax.rem(at + 2, 4)
            for i, d in enumerate((1, 3)):
                copy = remote(
                    pband(s, h, q, far, i),
                    got_hop.at[s, h, q, i],
                    sems,
                    base2 + (s * 2 + q) * GATHER + h * 4 + i,
                    dev(d),
                )
                copy.start()
                copies.append(copy)
        return copies

    def second_reduce(s, q, firsts):
        copies = []
        for h in range(2):
            dev, at = (dev_z, z) if h == 0 else (dev_x, x)
            for i, d in enumerate((1, 3)):
                firsts[h * 2 + i].wait()
                to = lax.rem(at + d, 4)
                for j in range(2):
                    k = (to, 2 * i + j) if h == 0 else (2 * i + j, to)
                    value = part[s, h, q, k[0], k[1]].astype(F32)
                    part[s, h, q, k[0], k[1]] = (
                        value + got_hop[s, h, q, i, j].astype(F32)
                    ).astype(BF16)
                copy = remote(
                    pband(s, h, q, to),
                    got_full.at[s, h, q, i],
                    sems,
                    base2 + (s * 2 + q) * GATHER + h * 4 + 2 + i,
                    dev(d),
                )
                copy.start()
                copies.append(copy)
        return copies

    def third_reduce(s, q, seconds):
        copies = []
        for h in range(2):
            for i in range(2):
                seconds[h * 2 + i].wait()
            for j in range(4):
                kept = part[s, h, q, z, j] if h == 0 else part[s, h, q, j, x]
                total = kept.astype(F32)
                for i in range(2):
                    total = total + got_full[s, h, q, i, j].astype(F32)
                quad[s, h, q, j] = total.astype(BF16)
            dev, at = (dev_x, x) if h == 0 else (dev_z, z)
            for d in (1, 2, 3):
                copy = remote(
                    quad.at[s, h, q, lax.rem(at + d, 4)],
                    got_quad.at[s, h, q, d - 1],
                    sems,
                    base2 + (s * 2 + q) * GATHER + 8 + h * 3 + d - 1,
                    dev(d),
                )
                copy.start()
                copies.append(copy)
        return copies

    base3 = base2 + 4 * GATHER

    def send_back(s, thirds):
        pieces = []
        for h in range(2):
            for q in range(2):
                for copy in thirds[q][h * 3 : h * 3 + 3]:
                    copy.wait()
                at = x if h == 0 else z
                total = quad[s, h, q, at].astype(F32)
                for d in range(3):
                    total = total + got_quad[s, h, q, d].astype(F32)
                total = total.astype(BF16)
                pieces.extend((total[:, :512], total[:, 512:]))
        stack = jnp.concatenate(pieces, axis=0)
        value = jnp.dot(swap, stack, preferred_element_type=F32).astype(BF16)
        reply[s] = value.reshape(8, 16, 512)
        copies = []
        for d in range(1, 8):
            copy = remote(
                reply.at[s, lax.rem(e + d, 8)],
                returned.at[s, e],
                sems,
                base3 + s * 7 + d - 1,
                dev_e(d),
            )
            copy.start()
            copies.append(copy)
        returned[s, e] = reply[s, e]
        return copies

    row, col = (lax.broadcasted_iota(jnp.int32, (128, 128), d) for d in range(2))
    moved = row // 32 * 32 + row // 4 % 2 * 16 + row // 8 % 4 * 4 + row % 4
    turn = jnp.where(col == moved, 1.0, 0.0).astype(BF16)
    for s in range(2):
        left[s] = jnp.dot(turn, gated[s], preferred_element_type=F32).astype(BF16)
        for q in range(2):
            first[s, q] = product(s, other, q).astype(BF16)
    pl.semaphore_wait(barrier, len(friends))
    swap0 = mixer_swap(0)
    swap1 = mixer_swap(1)
    for s in range(2):
        for q in range(2):
            mine[s, q] = product(s, c, q)
    ones0 = mixer_first(0, swap0)
    ones1 = mixer_first(1, swap1)
    twos0 = mixer_second(0, ones0)
    twos1 = mixer_second(1, ones1)
    last0 = mixer_third(0, twos0)
    rows_out(0, last0)
    last1 = mixer_third(1, twos1)
    first0 = first_gather(0)
    rows_out(1, last1)
    second0 = second_gather(0, first0)
    first1 = first_gather(1)
    third0 = third_gather(0, second0)
    second1 = second_gather(1, first1)
    for copy in third0:
        copy.wait()
    for load in loads[:2]:
        load.wait()
    compute(0)
    third1 = third_gather(1, second1)
    loads[2].wait()
    project(0, 0)
    hop00 = first_reduce(0, 0)
    project(0, 1)
    hop01 = first_reduce(0, 1)
    full00 = second_reduce(0, 0, hop00)
    full01 = second_reduce(0, 1, hop01)
    for copy in third1:
        copy.wait()
    compute(1)
    project(1, 0)
    hop10 = first_reduce(1, 0)
    project(1, 1)
    hop11 = first_reduce(1, 1)
    quad00 = third_reduce(0, 0, full00)
    full10 = second_reduce(1, 0, hop10)
    quad01 = third_reduce(0, 1, full01)
    full11 = second_reduce(1, 1, hop11)
    back0 = send_back(0, (quad00, quad01))
    quad10 = third_reduce(1, 0, full10)
    quad11 = third_reduce(1, 1, full11)
    back1 = send_back(1, (quad10, quad11))
    for copy in back0 + back1:
        copy.wait()
    for s in range(2):
        replies = returned[s].reshape(128, 512)
        high = mixes[s].astype(BF16)
        low = (mixes[s] - high.astype(F32)).astype(BF16)
        value = jnp.dot(high, replies, preferred_element_type=F32)
        value = value + jnp.dot(low, replies, preferred_element_type=F32)
        for k in range(8):
            cols = slice(k * 512, (k + 1) * 512)
            total = residual[s, :, cols] + value[k * 8 : (k + 1) * 8]
            out[s, :, cols] = jnp.where(c == 0, total[:4], total[4:]).astype(BF16)


def expert_layer(gated, weight, ids, route, layer_in, gate, up, down):
    vmem = pl.BlockSpec(memory_space=pltpu.VMEM)
    hbm = pl.BlockSpec(memory_space=pl.ANY)
    count = 14 + 6 * GATHER + 14
    return pl.pallas_call(
        expert_kernel,
        out_shape=jax.ShapeDtypeStruct((2, 4, 4096), BF16),
        in_specs=[vmem] * 4 + [hbm] * 4,
        out_specs=vmem,
        scratch_shapes=[
            pltpu.VMEM((2, 32, 4096), BF16),
            pltpu.VMEM((2, 128, 128), BF16),
            pltpu.VMEM((2, 2, 128, 1024), BF16),
            pltpu.VMEM((2, 2, 128, 1024), F32),
            pltpu.VMEM((2, 2, 128, 1024), BF16),
            pltpu.VMEM((2, 2, 4, 4, 16, 512), BF16),
            pltpu.VMEM((2, 2, 3, 4, 16, 512), BF16),
            pltpu.VMEM((2, 2, 4, 16, 512), BF16),
            pltpu.VMEM((2, 2, 3, 16, 512), BF16),
            pltpu.VMEM((2, 2, 16, 512), F32),
            pltpu.VMEM((2, 2, 16, 512), F32),
            pltpu.VMEM((2, 8, 4096), F32),
            pltpu.VMEM((512, 4096), BF16),
            pltpu.VMEM((512, 4096), BF16),
            pltpu.VMEM((512, 4096), BF16),
            pltpu.VMEM((2, 8, 16, 512), BF16),
            pltpu.VMEM((2, 8, 16, 512), BF16),
            pltpu.VMEM((2, 2, 4, 4, 16, 2048), BF16),
            pltpu.VMEM((256, 512), BF16),
            pltpu.VMEM((2, 2, 2, 4, 4, 16, 1024), BF16),
            pltpu.VMEM((2, 2, 2, 2, 2, 16, 1024), BF16),
            pltpu.VMEM((2, 2, 2, 2, 4, 16, 1024), BF16),
            pltpu.VMEM((2, 2, 2, 4, 16, 1024), BF16),
            pltpu.VMEM((2, 2, 2, 3, 16, 1024), BF16),
            pltpu.VMEM((2, 8, 16, 512), BF16),
            pltpu.VMEM((2, 8, 16, 512), BF16),
            pltpu.SemaphoreType.DMA((4,)),
            pltpu.SemaphoreType.DMA((count,)),
            pltpu.SemaphoreType.DMA((count,)),
            pltpu.SemaphoreType.DMA((30,)),
            pltpu.SemaphoreType.DMA((30,)),
        ],
        compiler_params=pltpu.CompilerParams(
            collective_id=1, has_side_effects=True, vmem_limit_bytes=58 * MIB
        ),
        name="experts",
    )(gated, weight, ids, route, layer_in, gate, up, down)


def shards(
    layer_in,
    conv_state,
    ssm_state,
    proj_inner,
    proj_gate,
    conv_weight,
    conv_bias,
    delta_down,
    state_proj,
    delta_up,
    delta_bias,
    decay_log,
    skip_gain,
    proj_out,
    expert_gate,
    expert_up,
    expert_down,
    expert_ids,
    route_weight,
):
    conv_in, activated, gate_branch, step_size, state_in = mixer_in(
        layer_in.reshape(256, 4096),
        proj_inner,
        proj_gate,
        jnp.transpose(conv_state, (1, 0, 2)),
        conv_weight,
        conv_bias[None],
        delta_down,
        state_proj.reshape(32, 128),
        delta_up,
        delta_bias[None],
    )
    conv_final = jnp.stack([conv_state[:, 2], conv_in[:128], conv_in[128:]], axis=1)
    step_size = step_size.reshape(2, 128, 128)
    state_in = state_in.reshape(2, 128, 32)
    rates = jnp.exp(decay_log)[None]
    act_float = activated.astype(F32).reshape(2, 128, 128)
    gate_branch = gate_branch.reshape(2, 128, 128)
    gated = []
    for s in range(2):
        size = step_size[s][:, None, :]
        ssm_state = (
            jnp.exp(-size * rates) * ssm_state
            + size * state_in[s, :, :16, None] * act_float[s][:, None, :]
        )
        readout = jnp.sum(ssm_state * state_in[s, :, 16:, None], axis=1)
        gated.append(
            ((readout + skip_gain * act_float[s]) * gate_branch[s]).astype(BF16)
        )
    layer_out = expert_layer(
        jnp.stack(gated),
        proj_out,
        expert_ids,
        route_weight,
        layer_in,
        expert_gate,
        expert_up,
        expert_down,
    )
    return (layer_out, conv_final, ssm_state)


def solution(mesh):
    channels = ("expert", "tensor")
    rows = ("dp", "expert", "tensor")
    placed = (
        P(None, "dp", None),
        P("dp", None, channels),
        P("dp", None, channels),
        P(None, channels),
        P(None, channels),
        P(None, channels),
        P(channels),
        P(channels, None),
        P(None, None, channels),
        P(None, channels),
        P(channels),
        P(None, channels),
        P(channels),
        P(channels, None),
        P("expert", ("dp", "tensor"), None),
        P("expert", ("dp", "tensor"), None),
        P("expert", ("dp", "tensor"), None),
        P(None, rows, None),
        P(None, rows, None),
    )
    return jax.shard_map(
        shards,
        mesh=mesh,
        in_specs=placed,
        out_specs=(P(None, rows, None), P("dp", None, channels), P("dp", None, channels)),
        check_vma=False,
    )
```

time: 134 us -> 118 us (0.88)
  local copies, waits for them, and re-layouts: 11.4 us -> 4.68 us
  Pallas kernels: 110 us -> 106 us
  other arithmetic: 9.45 us -> 5.58 us
  matrix products: 1.92 us -> 0 us
    select_n x2 -> x0, local copies, waits for them, and re-layouts: 4.61 us -> none  [tables(): mix = jnp.where(mask, weights, 0.0).reshape(256, 64).T]
    pallas_call x3 -> x2, Pallas kernels: 110 us -> 106 us  [the longest x1 84.1 us: expert_layer(): pl.pallas_call(expert_kernel, out_shape=jax.ShapeDtypeStruct((2, 4, 4096)...]
    reduce_sum x3 -> x0, other arithmetic: 2.41 us -> none  [the longest x1 2.23 us: shards(): jnp.mean(flat_float * flat_float, axis=-1, keepdims=True) + 1e-06]
    dot_general x5 -> x0, matrix products: 1.92 us -> none  [the longest x1 0.71 us: shards(): jnp.dot(flat, proj_inner, preferred_element_type=F32) * scale]
    convert_element_type x6 -> x1, other arithmetic: 1.65 us -> 0.03 us  [shards(): ((readout + skip_gain * act_float[s]) * gate_branch[s]).astype(BF16)]
    select_n x1 -> x0, other arithmetic: 1.56 us -> none  [tables(): mix = jnp.where(mask, weights, 0.0).reshape(256, 64).T]
    unnamed x42 -> x17, local copies, waits for them, and re-layouts: 3.27 us -> 2.88 us
where the time goes in v2:
time: 118 us; the launch traced here: 117 us
  Pallas kernels  106 us (90%)
  other arithmetic  5.58 us (5%)
  local copies, waits for them, and re-layouts  4.68 us (4%)
    pallas_call x1, Pallas kernels, expert_layer(): pl.pallas_call(expert_kernel, out_shape=jax.ShapeDtypeStruct((2, 4, 4096)...  84.1 us
    pallas_call x1, Pallas kernels, mixer_in(): pl.pallas_call(mixer_in_kernel, out_shape=(jax.ShapeDtypeStruct((256, 128...  22.3 us
    unnamed x17, local copies, waits for them, and re-layouts  2.88 us
    reduce_sum x1, other arithmetic, shards(): readout = jnp.sum(ssm_state * state_in[s, :, 16:, None], axis=1)  2.47 us

profile of v2, /device:TPU:1, one launch (start us, length us, event | category | flops | bytes accessed | tf_op | source)
XLA Modules:
  0.0 117.4 jit_solution(5305315287762277270)
XLA Ops:
  0.6 0.0 copy-start.3
  0.6 0.0 copy-start
  0.7 0.0 copy-start.6
  0.7 0.0 copy-start.4
  0.7 0.0 copy-start.5
  0.7 22.3 %mixer_in.1 = (bf16[256,128]{1,0:T(8,128)(2,1)}, bf16[256,128]{1,0:T(8,128)(2,1)}, f32[256,128]{1,0:T(8,128)}, f32[256,128]{1,0:T(8,128)}, f32[256,32]{1,0:T(8,128)}) custom-call(bf16[256,4096]{1,0:T(8,128)(2,1)} %bitcast.22, bf16[4096,128]{1,0:T(8,128)(2,1)} %inner_hbm.1, bf16[4096,128]{1,0:T(8,128)(2,1)} %gate_hbm.2, bf16[3,128,128]{2,1,0:T(8,128)(2,1)} %bitcast.24, ...), custom_call_target="tpu_custom_call" | custom-call | tf_op jit(solution)/shard_map/mixer_in/pallas_call | solution.py:192
  23.0 0.0 copy-start.1
  23.0 0.9 slice_negate_fusion
  23.9 1.0 slice_bitcast_fusion.2
  25.0 0.0 copy-done.3
  25.0 0.0 copy-done
  25.0 2.5 %multiply_reduce_fusion = (f32[128,128]{1,0:T(8,128)S(1)}, f32[128,16,128]{2,1,0:T(8,128)}, f32[128,128]{1,0:T(8,128)S(1)}) fusion(f32[128,16]{1,0:T(8,128)S(1)} %get-tuple-element.19, f32[128,128]{1,0:T(8,128)S(1)} %get-tuple-element.30, f32[128,16]{1,0:T(8,128)S(1)} %get-tuple-element.20, f32[128,128]{1,0:T(8,128)S(1)} %get-tuple-element.24, ...), kind=kLoop, calls=%fused_computation | loop fusion | flops 3637248 | bytes 2662400 | tf_op jit(solution)/shard_map/reduce_sum | solution.py:760
  27.5 0.8 convert_element_type.17
  28.3 0.0 copy-done.6
  28.3 0.0 copy-done.1
  28.4 0.6 pad_maximum_fusion.1.gated
  29.0 0.0 copy-done.4
  29.0 0.7 copy.22.ids
  29.7 0.0 copy-done.5
  29.7 0.7 copy.23.route
  30.4 0.0 copy-start.2
  30.4 84.1 %experts.1 = bf16[2,4,4096]{2,1,0:T(4,128)(2,1)} custom-call(bf16[2,128,128]{2,1,0:T(8,128)(2,1)} %pad_maximum_fusion.1.gated, bf16[128,4096]{1,0:T(8,128)(2,1)} %weight.1, s32[2,4,2]{2,1,0:T(4,128)} %copy.22.ids, f32[2,4,2]{2,1,0:T(4,128)} %copy.23.route, bf16[2,128,4096]{2,1,0:T(8,128)(2,1)} %layer_hbm.1, bf16[1,512,4096]{2,1,0:T(8,128)(2,1)} %gate_hbm.3, ...), custom_call_target="tpu_custom_call" | custom-call | tf_op jit(solution)/shard_map/experts/pallas_call | solution.py:669
  114.5 0.0 copy-done.2
  114.5 0.8 slice.57
  115.3 0.7 pad_maximum_fusion
  116.0 1.5 %copy.25 = bf16[2,4,4096]{2,1,0:T(4,128)(2,1)} copy(bf16[2,4,4096]{2,1,0:T(4,128)(2,1)} %experts.1) | data formatting | bytes 131072
  (3 shorter events, 0.0 us)
Async XLA Ops:
  0.6 24.3 %copy-start.3 = (f32[16,128]{1,0:T(8,128)S(1)}, f32[16,128]{1,0:T(8,128)}, u32[]{:S(2)}) copy-start(f32[16,128]{1,0:T(8,128)} %param.30) | copy-start | bytes 24580
  0.6 24.4 %copy-start = (f32[128,16,128]{2,1,0:T(8,128)S(1)}, f32[128,16,128]{2,1,0:T(8,128)}, u32[]{:S(2)}) copy-start(f32[128,16,128]{2,1,0:T(8,128)} %param.21) | copy-start | bytes 3145732
  0.7 27.7 %copy-start.6 = (f32[128]{0:T(128)S(1)}, f32[128]{0:T(128)}, u32[]{:S(2)}) copy-start(f32[128]{0:T(128)} %param.31) | copy-start | bytes 1540
  0.7 28.4 %copy-start.4 = (s32[2,4,2]{1,2,0:T(2,128)S(1)}, s32[2,4,2]{1,2,0:T(2,128)}, u32[]{:S(2)}) copy-start(s32[2,4,2]{1,2,0:T(2,128)} %param.36) | copy-start | bytes 196
  0.7 29.0 %copy-start.5 = (f32[2,4,2]{1,2,0:T(2,128)S(1)}, f32[2,4,2]{1,2,0:T(2,128)}, u32[]{:S(2)}) copy-start(f32[2,4,2]{1,2,0:T(2,128)} %param.37) | copy-start | bytes 196
  23.0 5.4 %copy-start.1 = (f32[256,128]{1,0:T(8,128)S(1)}, f32[256,128]{1,0:T(8,128)}, u32[]{:S(2)}) copy-start(f32[256,128]{1,0:T(8,128)} %get-tuple-element.11) | copy-start | bytes 393220
  30.4 84.1 %copy-start.2 = (bf16[256,128]{1,0:T(8,128)(2,1)S(1)}, bf16[256,128]{1,0:T(8,128)(2,1)}, u32[]{:S(2)}) copy-start(bf16[256,128]{1,0:T(8,128)(2,1)} %get-tuple-element.12) | copy-start | bytes 196612

commit v3 on v2

--- a/solution.py
+++ b/solution.py
@@ -96,7 +96,9 @@
         squares = squares + jnp.sum(wide * wide, axis=1, keepdims=True)
     scale = lax.rsqrt(squares * (1.0 / 4096) + 1e-06)
     conv_in = (conv_in * scale).astype(BF16)
-    conv_out[...] = conv_in
+    conv_out[0] = conv_state[2]
+    conv_out[1] = conv_in[:128]
+    conv_out[2] = conv_in[128:]
     conv_in = conv_in.astype(F32)
     window = [conv_state[k].astype(F32) for k in range(3)] + [conv_in[:128], conv_in[128:]]
     acts = []
@@ -183,7 +185,7 @@
     value = jnp.dot(normed, delta_up[...], preferred_element_type=F32) + delta_bias[...]
     size_out[...] = jnp.maximum(value, 0.0) + jnp.log1p(jnp.exp(-jnp.abs(value)))
     state = summed[:, 8:].reshape(256, 256)
-    state_out[...] = state[:, :32] + state[:, 32:64]
+    state_out[...] = state[:, :64].astype(BF16)
 
 
 def mixer_in(rows, inner, gate, *rest):
@@ -192,11 +194,11 @@
     return pl.pallas_call(
         mixer_in_kernel,
         out_shape=(
-            jax.ShapeDtypeStruct((256, 128), BF16),
+            jax.ShapeDtypeStruct((3, 128, 128), BF16),
             jax.ShapeDtypeStruct((256, 128), BF16),
             jax.ShapeDtypeStruct((256, 128), F32),
             jax.ShapeDtypeStruct((256, 128), F32),
-            jax.ShapeDtypeStruct((256, 32), F32),
+            jax.ShapeDtypeStruct((256, 64), BF16),
         ),
         in_specs=[hbm] * 3 + [vmem] * len(rest),
         out_specs=(vmem,) * 5,
@@ -224,9 +226,70 @@
     )(rows, inner, gate, *rest)
 
 
+BLOCK = 32
+
+
+def recurrence_kernel(size, act, gate, state_in, decay_log, skip, before, gated, after):
+    rates = jnp.exp(decay_log[...])[None]
+    held = before[...]
+    long = BLOCK * 16
+    row, col = (lax.broadcasted_iota(jnp.int32, (long, BLOCK), d) for d in range(2))
+    copy = jnp.where(row // 16 == col, 1.0, 0.0).astype(BF16)
+    row, col = (lax.broadcasted_iota(jnp.int32, (long, 64), d) for d in range(2))
+    masks = [jnp.where(col % 32 == k * 16 + row % 16, 1.0, 0.0) for k in range(2)]
+    ones = jnp.ones((64, 128), BF16)
+    for s in range(2):
+        spread = jnp.dot(copy, state_in[s], preferred_element_type=F32)
+        b_in, c_out = (
+            jnp.dot((spread * m).astype(BF16), ones, preferred_element_type=F32).reshape(
+                BLOCK, 16, 128
+            )
+            for m in masks
+        )
+        step = size[s]
+        x = act[s].astype(F32)
+        held = (
+            jnp.exp(-step[:, None, :] * rates) * held + (step * x)[:, None, :] * b_in
+        )
+        readout = jnp.sum(held * c_out, axis=1)
+        gated[s] = ((readout + skip[...] * x) * gate[s]).astype(BF16)
+    after[...] = held
+
+
+def recurrence(size, act, gate, state_in, decay_log, skip, before):
+    rows = pl.BlockSpec((2, BLOCK, 128), lambda i: (0, i, 0))
+    state = pl.BlockSpec((BLOCK, 16, 128), lambda i: (i, 0, 0))
+    return pl.pallas_call(
+        recurrence_kernel,
+        grid=(128 // BLOCK,),
+        out_shape=(
+            jax.ShapeDtypeStruct((2, 128, 128), BF16),
+            jax.ShapeDtypeStruct((128, 16, 128), F32),
+        ),
+        in_specs=[
+            rows,
+            rows,
+            rows,
+            pl.BlockSpec((2, BLOCK, 64), lambda i: (0, i, 0)),
+            pl.BlockSpec((16, 128), lambda i: (0, 0)),
+            pl.BlockSpec((1, 128), lambda i: (0, 0)),
+            state,
+        ],
+        out_specs=(rows, state),
+        compiler_params=pltpu.CompilerParams(vmem_limit_bytes=60 * MIB),
+        name="recurrence",
+    )(size, act, gate, state_in, decay_log, skip, before)
+
+
 def tables(ids, route, core):
+    row, col = (lax.broadcasted_iota(jnp.int32, (8, 4), d) for d in range(2))
+    own = row % 4 == col
+    ids, route = (
+        [jnp.sum(jnp.where(own, v[j : j + 1], 0), axis=1, keepdims=True) for j in range(2)]
+        for v in (ids, route)
+    )
     lane = lax.broadcasted_iota(jnp.int32, (8, 128), 1)
-    named = [lane == ids[:, j : j + 1] for j in range(2)]
+    named = [lane == ids[j] for j in range(2)]
     hit = (named[0] | named[1]).astype(F32)
     row, col = (lax.broadcasted_iota(jnp.int32, (8, 8), d) for d in range(2))
     earlier = ((col < row) & (col // 4 == row // 4)).astype(F32)
@@ -236,9 +299,9 @@
     pick, mix = None, None
     for j in range(2):
         slot = jnp.sum(jnp.where(named[j], count, 0.0), axis=1, keepdims=True).astype(jnp.int32)
-        target = jnp.where(here, ids[:, j : j + 1] * 16 + slot, -64)
+        target = jnp.where(here, ids[j] * 16 + slot, -64)
         mask = at == jnp.concatenate([target + 2 * k for k in range(8)], axis=0)
-        weight = jnp.concatenate([route[:, j : j + 1]] * 8, axis=0)
+        weight = jnp.concatenate([route[j]] * 8, axis=0)
         one = jnp.where(mask, 1.0, 0.0)
         pick = one if j == 0 else pick + one
         mix = one * weight if j == 0 else mix + one * weight
@@ -251,7 +314,8 @@
     return jnp.where(col == swapped, 1.0, 0.0).astype(BF16)
 
 
-GATHER = 14
+GATHER = 22
+REDUCE = 14
 
 
 def expert_kernel(
@@ -265,11 +329,6 @@
     e = y * 2 + c
     sems = (ss, rs)
     mixer_sems = (mss, mrs)
-    loads = []
-    for i, (a, b) in enumerate(((gate_hbm, gate), (up_hbm, up), (down_hbm, down))):
-        load = pltpu.make_async_copy(a.at[0], b, local.at[i])
-        load.start()
-        loads.append(load)
     chip_rows = pltpu.make_async_copy(
         layer_hbm.at[:, pl.ds(pl.multiple_of(y * 32, 32), 32)], own, local.at[3]
     )
@@ -367,19 +426,7 @@
         copy.start()
         return copy
 
-    picks, mixes = [], []
-    for s in range(2):
-        pick, mix = tables(
-            jnp.concatenate([ids[s]] * 2, axis=0), jnp.concatenate([route[s]] * 2, axis=0), c
-        )
-        picks.append(pick)
-        mixes.append(mix)
-    swap = swap_fields()
-
-    sends = {}
-
-    row, col = (lax.broadcasted_iota(jnp.int32, (16, 32), d) for d in range(2))
-    chosen = jnp.where(col == row // 4 * 16 + x * 4 + row % 4, 1.0, 0.0).astype(BF16)
+    picks, mixes, helpers, sends = [], [], [], {}
 
     def rows_out(s, copy):
         if s == 0:
@@ -390,7 +437,7 @@
             for q in range(2):
                 for k in range(2):
                     cols = pl.ds(pl.multiple_of(half * 2048 + q * 1024 + k * 512, 512), 512)
-                    step_rows = jnp.dot(chosen, own[s, :, cols], preferred_element_type=F32)
+                    step_rows = jnp.dot(helpers[1], own[s, :, cols], preferred_element_type=F32)
                     residual[s, :, cols] = source[s, q, k * 8 : k * 8 + 8] + step_rows[:8]
         value = residual[s]
         normed = value * lax.rsqrt(jnp.mean(value * value, axis=-1, keepdims=True) + 1e-06)
@@ -412,13 +459,13 @@
         arrived[s, e] = message[s, e]
 
     base = 14
-    halves = (pl.ds(0, 2048), pl.ds(2048, 2048))
+    halves = (slice(0, 2048), slice(2048, 4096))
 
     def first_gather(s):
         for d in range(1, 8):
             sends[s, d].wait()
         ordered = jnp.dot(
-            swap, arrived[s].reshape(128, 512), preferred_element_type=F32
+            helpers[0], arrived[s].reshape(128, 512), preferred_element_type=F32
         ).astype(BF16)
         for k in range(8):
             h, at = divmod(k, 4)
@@ -437,54 +484,51 @@
                 copies.append(copy)
         return copies
 
-    def band(s, h, at, half=None):
+    def band(s, h, q, at, half=None):
         along = pl.ds(0, 4) if half is None else pl.ds(2 * half, 2)
-        return rows.at[s, h, at, along] if h == 0 else rows.at[s, h, along, at]
+        every, cols = slice(None), pl.ds(q * 1024, 1024)
+        at = (at, along) if h == 0 else (along, at)
+        return rows.at[(s, h, *at, every, cols)]
 
     def second_gather(s, firsts):
+        copies = {}
+        for q in range(2):
+            for h in range(2):
+                if q == 0:
+                    for copy in firsts[h * 3 : h * 3 + 3]:
+                        copy.wait()
+                dev, at = (dev_z, z) if h == 0 else (dev_x, x)
+                for i, d in enumerate((1, 3)):
+                    mine_ = band(s, h, q, at)
+                    n = base + s * GATHER + 6 + q * 8 + h * 4 + i
+                    copy = remote(mine_, mine_, sems, n, dev(d))
+                    copy.start()
+                    copies[q, h, i] = copy
+        return copies
+
+    def third_gather(s, q, seconds):
         copies = []
-        at0 = base + s * GATHER + 6
-        for h in range(2):
-            for copy in firsts[h * 3 : h * 3 + 3]:
-                copy.wait()
-            dev, at = (dev_z, z) if h == 0 else (dev_x, x)
-            for i, d in enumerate((1, 3)):
-                copy = remote(band(s, h, at), band(s, h, at), sems, at0 + h * 4 + i, dev(d))
-                copy.start()
-                copies.append(copy)
-        return copies
-
-    def third_gather(s, seconds):
-        copies = []
-        at0 = base + s * GATHER + 6
         for h in range(2):
             dev, at = (dev_z, z) if h == 0 else (dev_x, x)
             for i, d in enumerate((1, 3)):
-                seconds[h * 2 + i].wait()
-                source = lax.rem(at + 4 - d, 4)
-                copy = remote(
-                    band(s, h, source, i), band(s, h, source, i), sems, at0 + h * 4 + 2 + i, dev(d)
-                )
+                seconds[q, h, i].wait()
+                piece = band(s, h, q, lax.rem(at + 4 - d, 4), i)
+                n = base + s * GATHER + 6 + q * 8 + h * 4 + 2 + i
+                copy = remote(piece, piece, sems, n, dev(d))
                 copy.start()
                 copies.append(copy)
         return copies
 
-    def compute(s):
-        wide = 256
-
-        def hidden(t, carry):
-            at = pl.ds(pl.multiple_of(t * wide, wide), wide)
-            g = jnp.zeros((256, wide), F32)
-            u = jnp.zeros((256, wide), F32)
-            for h in range(2):
-                piece = rows[s, h].reshape(256, 2048)
-                nt = (((1,), (1,)), ((), ()))
-                g = g + lax.dot_general(piece, gate[at, halves[h]], nt, preferred_element_type=F32)
-                u = u + lax.dot_general(piece, up[at, halves[h]], nt, preferred_element_type=F32)
-            act[:, at] = (g / (1.0 + jnp.exp(-g)) * u).astype(BF16)
-            return carry
-
-        lax.fori_loop(0, 512 // wide, hidden, 0)
+    def compute(s, t):
+        at = slice(t * 256, (t + 1) * 256)
+        g = jnp.zeros((256, 256), F32)
+        u = jnp.zeros((256, 256), F32)
+        for h in range(2):
+            piece = rows[s, h].reshape(256, 2048)
+            nt = (((1,), (1,)), ((), ()))
+            g = g + lax.dot_general(piece, gate[at, halves[h]], nt, preferred_element_type=F32)
+            u = u + lax.dot_general(piece, up[at, halves[h]], nt, preferred_element_type=F32)
+        act[:, at] = (silu(g) * u).astype(BF16)
 
     def project(s, q):
         for h in range(2):
@@ -508,7 +552,7 @@
                     pband(s, h, q, far, i),
                     got_hop.at[s, h, q, i],
                     sems,
-                    base2 + (s * 2 + q) * GATHER + h * 4 + i,
+                    base2 + (s * 2 + q) * REDUCE + h * 4 + i,
                     dev(d),
                 )
                 copy.start()
@@ -532,7 +576,7 @@
                     pband(s, h, q, to),
                     got_full.at[s, h, q, i],
                     sems,
-                    base2 + (s * 2 + q) * GATHER + h * 4 + 2 + i,
+                    base2 + (s * 2 + q) * REDUCE + h * 4 + 2 + i,
                     dev(d),
                 )
                 copy.start()
@@ -556,14 +600,14 @@
                     quad.at[s, h, q, lax.rem(at + d, 4)],
                     got_quad.at[s, h, q, d - 1],
                     sems,
-                    base2 + (s * 2 + q) * GATHER + 8 + h * 3 + d - 1,
+                    base2 + (s * 2 + q) * REDUCE + 8 + h * 3 + d - 1,
                     dev(d),
                 )
                 copy.start()
                 copies.append(copy)
         return copies
 
-    base3 = base2 + 4 * GATHER
+    base3 = base2 + 4 * REDUCE
 
     def send_back(s, thirds):
         pieces = []
@@ -578,7 +622,7 @@
                 total = total.astype(BF16)
                 pieces.extend((total[:, :512], total[:, 512:]))
         stack = jnp.concatenate(pieces, axis=0)
-        value = jnp.dot(swap, stack, preferred_element_type=F32).astype(BF16)
+        value = jnp.dot(helpers[0], stack, preferred_element_type=F32).astype(BF16)
         reply[s] = value.reshape(8, 16, 512)
         copies = []
         for d in range(1, 8):
@@ -597,18 +641,32 @@
     row, col = (lax.broadcasted_iota(jnp.int32, (128, 128), d) for d in range(2))
     moved = row // 32 * 32 + row // 4 % 2 * 16 + row // 8 % 4 * 4 + row % 4
     turn = jnp.where(col == moved, 1.0, 0.0).astype(BF16)
+    swaps = []
     for s in range(2):
         left[s] = jnp.dot(turn, gated[s], preferred_element_type=F32).astype(BF16)
         for q in range(2):
             first[s, q] = product(s, other, q).astype(BF16)
-    pl.semaphore_wait(barrier, len(friends))
-    swap0 = mixer_swap(0)
-    swap1 = mixer_swap(1)
+        if s == 0:
+            pl.semaphore_wait(barrier, len(friends))
+        swaps.append(mixer_swap(s))
     for s in range(2):
         for q in range(2):
             mine[s, q] = product(s, c, q)
-    ones0 = mixer_first(0, swap0)
-    ones1 = mixer_first(1, swap1)
+    ones0 = mixer_first(0, swaps[0])
+    ones1 = mixer_first(1, swaps[1])
+    for s in range(2):
+        pick, mix = tables(ids[s], route[s], c)
+        picks.append(pick)
+        mixes.append(mix)
+    swap = swap_fields()
+    row, col = (lax.broadcasted_iota(jnp.int32, (16, 32), d) for d in range(2))
+    chosen = jnp.where(col == row // 4 * 16 + x * 4 + row % 4, 1.0, 0.0).astype(BF16)
+    helpers.extend((swap, chosen))
+    loads = []
+    for i, (a, b) in enumerate(((gate_hbm, gate), (up_hbm, up), (down_hbm, down))):
+        load = pltpu.make_async_copy(a.at[0], b, local.at[i])
+        load.start()
+        loads.append(load)
     twos0 = mixer_second(0, ones0)
     twos1 = mixer_second(1, ones1)
     last0 = mixer_third(0, twos0)
@@ -618,31 +676,35 @@
     rows_out(1, last1)
     second0 = second_gather(0, first0)
     first1 = first_gather(1)
-    third0 = third_gather(0, second0)
+    third00 = third_gather(0, 0, second0)
+    third01 = third_gather(0, 1, second0)
     second1 = second_gather(1, first1)
-    for copy in third0:
+    for copy in third00 + third01:
         copy.wait()
     for load in loads[:2]:
         load.wait()
-    compute(0)
-    third1 = third_gather(1, second1)
+    compute(0, 0)
+    third10 = third_gather(1, 0, second1)
+    compute(0, 1)
     loads[2].wait()
     project(0, 0)
     hop00 = first_reduce(0, 0)
+    third11 = third_gather(1, 1, second1)
     project(0, 1)
     hop01 = first_reduce(0, 1)
     full00 = second_reduce(0, 0, hop00)
     full01 = second_reduce(0, 1, hop01)
-    for copy in third1:
+    for copy in third10 + third11:
         copy.wait()
-    compute(1)
+    compute(1, 0)
+    compute(1, 1)
     project(1, 0)
     hop10 = first_reduce(1, 0)
+    quad00 = third_reduce(0, 0, full00)
     project(1, 1)
     hop11 = first_reduce(1, 1)
-    quad00 = third_reduce(0, 0, full00)
+    quad01 = third_reduce(0, 1, full01)
     full10 = second_reduce(1, 0, hop10)
-    quad01 = third_reduce(0, 1, full01)
     full11 = second_reduce(1, 1, hop11)
     back0 = send_back(0, (quad00, quad01))
     quad10 = third_reduce(1, 0, full10)
@@ -659,16 +721,16 @@
         for k in range(8):
             cols = slice(k * 512, (k + 1) * 512)
             total = residual[s, :, cols] + value[k * 8 : (k + 1) * 8]
-            out[s, :, cols] = jnp.where(c == 0, total[:4], total[4:]).astype(BF16)
+            out[s, :, cols] = jnp.where(c == 0, total[:4], total[4:])
 
 
 def expert_layer(gated, weight, ids, route, layer_in, gate, up, down):
     vmem = pl.BlockSpec(memory_space=pltpu.VMEM)
     hbm = pl.BlockSpec(memory_space=pl.ANY)
-    count = 14 + 6 * GATHER + 14
+    count = 14 + 2 * GATHER + 4 * REDUCE + 14
     return pl.pallas_call(
         expert_kernel,
-        out_shape=jax.ShapeDtypeStruct((2, 4, 4096), BF16),
+        out_shape=jax.ShapeDtypeStruct((2, 4, 4096), F32),
         in_specs=[vmem] * 4 + [hbm] * 4,
         out_specs=vmem,
         scratch_shapes=[
@@ -732,7 +794,7 @@
     expert_ids,
     route_weight,
 ):
-    conv_in, activated, gate_branch, step_size, state_in = mixer_in(
+    conv_final, activated, gate_branch, step_size, state_in = mixer_in(
         layer_in.reshape(256, 4096),
         proj_inner,
         proj_gate,
@@ -744,34 +806,27 @@
         delta_up,
         delta_bias[None],
     )
-    conv_final = jnp.stack([conv_state[:, 2], conv_in[:128], conv_in[128:]], axis=1)
-    step_size = step_size.reshape(2, 128, 128)
-    state_in = state_in.reshape(2, 128, 32)
-    rates = jnp.exp(decay_log)[None]
-    act_float = activated.astype(F32).reshape(2, 128, 128)
-    gate_branch = gate_branch.reshape(2, 128, 128)
-    gated = []
-    for s in range(2):
-        size = step_size[s][:, None, :]
-        ssm_state = (
-            jnp.exp(-size * rates) * ssm_state
-            + size * state_in[s, :, :16, None] * act_float[s][:, None, :]
-        )
-        readout = jnp.sum(ssm_state * state_in[s, :, 16:, None], axis=1)
-        gated.append(
-            ((readout + skip_gain * act_float[s]) * gate_branch[s]).astype(BF16)
-        )
+    conv_final = jnp.transpose(conv_final, (1, 0, 2))
+    gated, ssm_state = recurrence(
+        step_size.reshape(2, 128, 128),
+        activated.reshape(2, 128, 128),
+        gate_branch.reshape(2, 128, 128),
+        state_in.reshape(2, 128, 64),
+        decay_log,
+        skip_gain[None],
+        ssm_state,
+    )
     layer_out = expert_layer(
-        jnp.stack(gated),
+        gated,
         proj_out,
-        expert_ids,
-        route_weight,
+        jnp.transpose(expert_ids, (0, 2, 1)),
+        jnp.transpose(route_weight, (0, 2, 1)),
         layer_in,
         expert_gate,
         expert_up,
         expert_down,
     )
-    return (layer_out, conv_final, ssm_state)
+    return (layer_out.astype(BF16), conv_final, ssm_state)
 
 
 def solution(mesh):

time: 118 us -> 113 us (0.958)
  local copies, waits for them, and re-layouts: 4.68 us -> 0.64 us
  other arithmetic: 5.58 us -> 1.56 us
  Pallas kernels: 106 us -> 110 us
    pallas_call x1 -> x2, Pallas kernels: 22.3 us -> 26.9 us  [the longest x1 22.2 us: mixer_in(): pl.pallas_call(mixer_in_kernel, out_shape=(jax.ShapeDtypeStruct((3, 128,...]
    reduce_sum x1 -> x0, other arithmetic: 2.47 us -> none  [shards(): readout = jnp.sum(ssm_state * state_in[s, :, 16:, None], axis=1)]
    unnamed x17 -> x3, local copies, waits for them, and re-layouts: 2.88 us -> 0.64 us
    another operation x2 -> x0, other arithmetic: 1.29 us -> none  [the longest x1 0.65 us: shards(): jnp.stack([conv_state[:, 2], conv_in[:128], conv_in[128:]], axis=1)]
where the time goes in v3:
time: 113 us
  Pallas kernels  110 us (97%)
  other arithmetic  1.56 us (1%)
    pallas_call x1, Pallas kernels, expert_layer(): pl.pallas_call(expert_kernel, out_shape=jax.ShapeDtypeStruct((2, 4, 4096)...  82.9 us
    pallas_call x1, Pallas kernels, mixer_in(): pl.pallas_call(mixer_in_kernel, out_shape=(jax.ShapeDtypeStruct((3, 128,...  22.2 us
    pallas_call x1, Pallas kernels, recurrence(): pl.pallas_call(recurrence_kernel, grid=(128 // BLOCK,), out_shape=(jax.Sh...  4.69 us

profile of v3, /device:TPU:1, one launch (start us, length us, event | category | flops | bytes accessed | tf_op | source)
XLA Modules:
  0.0 112.7 jit_solution(15471537578790259861)
XLA Ops:
  0.6 22.2 %mixer_in.1 = (bf16[3,128,128]{2,1,0:T(8,128)(2,1)}, bf16[256,128]{1,0:T(8,128)(2,1)}, f32[256,128]{1,0:T(8,128)}, f32[256,128]{1,0:T(8,128)}, bf16[256,64]{1,0:T(8,128)(2,1)}) custom-call(bf16[256,4096]{1,0:T(8,128)(2,1)} %bitcast.13, bf16[4096,128]{1,0:T(8,128)(2,1)} %inner_hbm.1, bf16[4096,128]{1,0:T(8,128)(2,1)} %gate_hbm.2, ...), custom_call_target="tpu_custom_call" | custom-call | tf_op jit(solution)/shard_map/mixer_in/pallas_call | solution.py:194
  22.8 4.7 %recurrence.1 = (bf16[2,128,128]{2,1,0:T(8,128)(2,1)}, f32[128,16,128]{2,1,0:T(8,128)}) custom-call(f32[2,128,128]{2,1,0:T(8,128)} %bitcast.15, bf16[2,128,128]{2,1,0:T(8,128)(2,1)} %bitcast.18, f32[2,128,128]{2,1,0:T(8,128)} %bitcast.14, bf16[2,128,64]{2,1,0:T(8,128)(2,1)} %bitcast.19, f32[16,128]{1,0:T(8,128)} %decay_log.1, f32[1,128]{1,0:T(1,128)} %bitcast.25, ...), custom_call_target="tpu_custom_call" | custom-call | tf_op jit(solution)/shard_map/recurrence/pallas_call | solution.py:262
  27.5 0.0 copy-start
  27.5 82.9 %experts.1 = f32[2,4,4096]{2,1,0:T(4,128)} custom-call(bf16[2,128,128]{2,1,0:T(8,128)(2,1)} %get-tuple-element.14.gated, bf16[128,4096]{1,0:T(8,128)(2,1)} %weight.1, s32[2,2,4]{2,1,0:T(2,128)} %bitcast.21, f32[2,2,4]{2,1,0:T(2,128)} %bitcast.22, bf16[2,128,4096]{2,1,0:T(8,128)(2,1)} %layer_hbm.1, bf16[1,512,4096]{2,1,0:T(8,128)(2,1)} %gate_hbm.3, ...), custom_call_target="tpu_custom_call" | custom-call | tf_op jit(solution)/shard_map/experts/pallas_call | solution.py:731
  110.5 1.6 %convert_element_type.3 = bf16[2,4,4096]{2,1,0:T(4,128)(2,1)} convert(f32[2,4,4096]{2,1,0:T(4,128)} %experts.1) | non-fusion elementwise | flops 32768 | bytes 196608 | tf_op jit(solution)/shard_map/convert_element_type | solution.py:829
  112.1 0.0 copy-done
  112.1 0.6 copy.23
Async XLA Ops:
  27.5 84.5 %copy-start = (bf16[3,128,128]{2,1,0:T(8,128)(2,1)S(1)}, bf16[3,128,128]{2,1,0:T(8,128)(2,1)}, u32[]{:S(2)}) copy-start(bf16[3,128,128]{2,1,0:T(8,128)(2,1)} %get-tuple-element.15) | copy-start | bytes 294916

commit v4 on v3

--- a/solution.py
+++ b/solution.py
@@ -41,32 +41,30 @@
 
 
 PIECES = 4
+SMALL = 7
 
 
 def mixer_in_kernel(
-    rows_hbm, inner_hbm, gate_hbm, conv_state, conv_weight, conv_bias, delta_down, state_proj,
-    delta_up, delta_bias,
-    conv_out, act_out, gate_out, size_out, state_out,
-    rows, inner, gate, local, part, got, both, recv, out, one, other, send_a, recv_a, send_b, recv_b,
+    rows_hbm, inner_hbm, gate_hbm, *refs
 ):
+    small_hbm, refs = refs[:SMALL], refs[SMALL:]
+    conv_out, act_out, gate_out, size_out, state_out = refs[:5]
+    small, refs = refs[5 : 5 + SMALL], refs[5 + SMALL :]
+    (
+    rows, inner, gate, local, part, got, both, recv, out, one, other, send_a, recv_a, send_b, recv_b
+    ) = refs
     z, y, c, x = place()
     me = y * 4 + x
     width = 4096 // PIECES
-    loads = []
-    for k in range(PIECES):
-        cut = pl.ds(k * width, width)
-        three = []
-        for i, (a, b) in enumerate(
-            (
-                (rows_hbm.at[:, cut], rows.at[:, cut]),
-                (inner_hbm.at[cut], inner.at[cut]),
-                (gate_hbm.at[cut], gate.at[cut]),
-            )
-        ):
-            load = pltpu.make_async_copy(a, b, local.at[k * 3 + i])
-            load.start()
-            three.append(load)
-        loads.append(three)
+    cuts = [pl.ds(k * width, width) for k in range(PIECES)]
+    pairs = [p for k in cuts for p in ((rows_hbm.at[:, k], rows.at[:, k]), (inner_hbm.at[k], inner.at[k]))]
+    pairs.extend(zip(small_hbm, small))
+    pairs.extend((gate_hbm.at[k], gate.at[k]) for k in cuts)
+    loads = [pltpu.make_async_copy(a, b, local.at[i]) for i, (a, b) in enumerate(pairs)]
+    for load in loads:
+        load.start()
+    conv_state, conv_weight, conv_bias, delta_down, state_proj, delta_up, delta_bias = small
+    small_loads, gate_loads = loads[2 * PIECES : 2 * PIECES + SMALL], loads[2 * PIECES + SMALL :]
 
     def chip(p):
         return (z, lax.div(p, 4) * 2 + c, lax.rem(p, 4))
@@ -86,8 +84,8 @@
     squares = jnp.zeros((256, 1), F32)
     conv_in = jnp.zeros((256, 128), F32)
     for k in range(PIECES):
-        loads[k][0].wait()
-        loads[k][1].wait()
+        loads[2 * k].wait()
+        loads[2 * k + 1].wait()
         piece = rows[:, k * width : (k + 1) * width]
         conv_in = conv_in + jnp.dot(
             piece, inner[k * width : (k + 1) * width], preferred_element_type=F32
@@ -95,6 +93,8 @@
         wide = piece.astype(F32)
         squares = squares + jnp.sum(wide * wide, axis=1, keepdims=True)
     scale = lax.rsqrt(squares * (1.0 / 4096) + 1e-06)
+    for load in small_loads:
+        load.wait()
     conv_in = (conv_in * scale).astype(BF16)
     conv_out[0] = conv_state[2]
     conv_out[1] = conv_in[:128]
@@ -135,7 +135,7 @@
 
     gated = jnp.zeros((256, 128), F32)
     for k in range(PIECES):
-        loads[k][2].wait()
+        gate_loads[k].wait()
         gated = gated + jnp.dot(
             rows[:, k * width : (k + 1) * width],
             gate[k * width : (k + 1) * width],
@@ -200,13 +200,14 @@
             jax.ShapeDtypeStruct((256, 128), F32),
             jax.ShapeDtypeStruct((256, 64), BF16),
         ),
-        in_specs=[hbm] * 3 + [vmem] * len(rest),
+        in_specs=[hbm] * (3 + len(rest)),
         out_specs=(vmem,) * 5,
         scratch_shapes=[
+            *(pltpu.VMEM(v.shape, v.dtype) for v in rest),
             pltpu.VMEM((256, 4096), BF16),
             pltpu.VMEM((4096, 128), BF16),
             pltpu.VMEM((4096, 128), BF16),
-            pltpu.SemaphoreType.DMA((3 * PIECES,)),
+            pltpu.SemaphoreType.DMA((3 * PIECES + SMALL,)),
             pltpu.VMEM((2, 16, 16, 256), BF16),
             pltpu.VMEM((16, 16, 256), BF16),
             pltpu.VMEM((16, 16, 256), BF16),
@@ -226,12 +227,13 @@
     )(rows, inner, gate, *rest)
 
 
-BLOCK = 32
-
-
-def recurrence_kernel(size, act, gate, state_in, decay_log, skip, before, gated, after):
+BLOCK = 64
+
+
+def recurrence_kernel(size, act, gate, state_in, decay_log, skip, conv, before, gated, after, conv_out):
     rates = jnp.exp(decay_log[...])[None]
     held = before[...]
+    conv_out[...] = conv[...]
     long = BLOCK * 16
     row, col = (lax.broadcasted_iota(jnp.int32, (long, BLOCK), d) for d in range(2))
     copy = jnp.where(row // 16 == col, 1.0, 0.0).astype(BF16)
@@ -256,7 +258,7 @@
     after[...] = held
 
 
-def recurrence(size, act, gate, state_in, decay_log, skip, before):
+def recurrence(size, act, gate, state_in, decay_log, skip, conv, before):
     rows = pl.BlockSpec((2, BLOCK, 128), lambda i: (0, i, 0))
     state = pl.BlockSpec((BLOCK, 16, 128), lambda i: (i, 0, 0))
     return pl.pallas_call(
@@ -265,6 +267,7 @@
         out_shape=(
             jax.ShapeDtypeStruct((2, 128, 128), BF16),
             jax.ShapeDtypeStruct((128, 16, 128), F32),
+            jax.ShapeDtypeStruct((3, 128, 128), BF16),
         ),
         in_specs=[
             rows,
@@ -273,12 +276,13 @@
             pl.BlockSpec((2, BLOCK, 64), lambda i: (0, i, 0)),
             pl.BlockSpec((16, 128), lambda i: (0, 0)),
             pl.BlockSpec((1, 128), lambda i: (0, 0)),
+            pl.BlockSpec((3, BLOCK, 128), lambda i: (0, i, 0)),
             state,
         ],
-        out_specs=(rows, state),
+        out_specs=(rows, state, pl.BlockSpec((3, BLOCK, 128), lambda i: (0, i, 0))),
         compiler_params=pltpu.CompilerParams(vmem_limit_bytes=60 * MIB),
         name="recurrence",
-    )(size, act, gate, state_in, decay_log, skip, before)
+    )(size, act, gate, state_in, decay_log, skip, conv, before)
 
 
 def tables(ids, route, core):
@@ -319,9 +323,9 @@
 
 
 def expert_kernel(
-    gated, weight, ids, route, layer_hbm, gate_hbm, up_hbm, down_hbm,
+    gated_hbm, weight_hbm, ids_hbm, route_hbm, layer_hbm, gate_hbm, up_hbm, down_hbm,
     out,
-    own, left, first, mine, got0, sums, got1, mid, got2, last, got3, residual,
+    gated, weight, ids, route, own, left, first, mine, got0, sums, got1, mid, got2, last, got3, residual,
     gate, up, down, message, arrived, rows, act, part, got_hop, got_full, quad, got_quad,
     reply, returned, local, ss, rs, mss, mrs,
 ):
@@ -329,11 +333,6 @@
     e = y * 2 + c
     sems = (ss, rs)
     mixer_sems = (mss, mrs)
-    chip_rows = pltpu.make_async_copy(
-        layer_hbm.at[:, pl.ds(pl.multiple_of(y * 32, 32), 32)], own, local.at[3]
-    )
-    chip_rows.start()
-
     def dev_e(d):
         return (z, lax.rem(e + d, 8), x)
 
@@ -351,6 +350,21 @@
     barrier = pltpu.get_barrier_semaphore()
     for friend in friends:
         pl.semaphore_signal(barrier, inc=1, device_id=friend, device_id_type=MESH)
+
+    early = [pltpu.make_async_copy(gated_hbm, gated, local.at[4])]
+    for i in range(2):
+        cols = pl.ds(pl.multiple_of(((1 - c) if i == 0 else c) * 2048, 2048), 2048)
+        early.append(
+            pltpu.make_async_copy(weight_hbm.at[:, cols], weight.at[:, cols], local.at[5 + i])
+        )
+    early.append(pltpu.make_async_copy(ids_hbm, ids, local.at[7]))
+    early.append(pltpu.make_async_copy(route_hbm, route, local.at[8]))
+    for load in early:
+        load.start()
+    chip_rows = pltpu.make_async_copy(
+        layer_hbm.at[:, pl.ds(pl.multiple_of(y * 32, 32), 32)], own, local.at[3]
+    )
+    chip_rows.start()
 
     MIXER = 15
     other = 1 - c
@@ -642,6 +656,8 @@
     moved = row // 32 * 32 + row // 4 % 2 * 16 + row // 8 % 4 * 4 + row % 4
     turn = jnp.where(col == moved, 1.0, 0.0).astype(BF16)
     swaps = []
+    early[0].wait()
+    early[1].wait()
     for s in range(2):
         left[s] = jnp.dot(turn, gated[s], preferred_element_type=F32).astype(BF16)
         for q in range(2):
@@ -649,11 +665,14 @@
         if s == 0:
             pl.semaphore_wait(barrier, len(friends))
         swaps.append(mixer_swap(s))
+    early[2].wait()
     for s in range(2):
         for q in range(2):
             mine[s, q] = product(s, c, q)
     ones0 = mixer_first(0, swaps[0])
     ones1 = mixer_first(1, swaps[1])
+    early[3].wait()
+    early[4].wait()
     for s in range(2):
         pick, mix = tables(ids[s], route[s], c)
         picks.append(pick)
@@ -710,9 +729,9 @@
     quad10 = third_reduce(1, 0, full10)
     quad11 = third_reduce(1, 1, full11)
     back1 = send_back(1, (quad10, quad11))
-    for copy in back0 + back1:
-        copy.wait()
     for s in range(2):
+        for copy in (back0, back1)[s]:
+            copy.wait()
         replies = returned[s].reshape(128, 512)
         high = mixes[s].astype(BF16)
         low = (mixes[s] - high.astype(F32)).astype(BF16)
@@ -731,9 +750,13 @@
     return pl.pallas_call(
         expert_kernel,
         out_shape=jax.ShapeDtypeStruct((2, 4, 4096), F32),
-        in_specs=[vmem] * 4 + [hbm] * 4,
+        in_specs=[hbm] * 8,
         out_specs=vmem,
         scratch_shapes=[
+            pltpu.VMEM((2, 128, 128), BF16),
+            pltpu.VMEM((128, 4096), BF16),
+            pltpu.VMEM((2, 2, 4), jnp.int32),
+            pltpu.VMEM((2, 2, 4), F32),
             pltpu.VMEM((2, 32, 4096), BF16),
             pltpu.VMEM((2, 128, 128), BF16),
             pltpu.VMEM((2, 2, 128, 1024), BF16),
@@ -760,17 +783,32 @@
             pltpu.VMEM((2, 2, 2, 3, 16, 1024), BF16),
             pltpu.VMEM((2, 8, 16, 512), BF16),
             pltpu.VMEM((2, 8, 16, 512), BF16),
-            pltpu.SemaphoreType.DMA((4,)),
+            pltpu.SemaphoreType.DMA((9,)),
             pltpu.SemaphoreType.DMA((count,)),
             pltpu.SemaphoreType.DMA((count,)),
             pltpu.SemaphoreType.DMA((30,)),
             pltpu.SemaphoreType.DMA((30,)),
         ],
         compiler_params=pltpu.CompilerParams(
-            collective_id=1, has_side_effects=True, vmem_limit_bytes=58 * MIB
+            collective_id=1, has_side_effects=True, vmem_limit_bytes=60 * MIB
         ),
         name="experts",
     )(gated, weight, ids, route, layer_in, gate, up, down)
+
+
+def finish_kernel(value, out):
+    out[...] = value[...].astype(BF16)
+
+
+def finish(value):
+    vmem = pl.BlockSpec(memory_space=pltpu.VMEM)
+    return pl.pallas_call(
+        finish_kernel,
+        out_shape=jax.ShapeDtypeStruct(value.shape, BF16),
+        in_specs=[vmem],
+        out_specs=vmem,
+        name="finish",
+    )(value)
 
 
 def shards(
@@ -806,16 +844,17 @@
         delta_up,
         delta_bias[None],
     )
-    conv_final = jnp.transpose(conv_final, (1, 0, 2))
-    gated, ssm_state = recurrence(
+    gated, ssm_state, conv_final = recurrence(
         step_size.reshape(2, 128, 128),
         activated.reshape(2, 128, 128),
         gate_branch.reshape(2, 128, 128),
         state_in.reshape(2, 128, 64),
         decay_log,
         skip_gain[None],
+        conv_final,
         ssm_state,
     )
+    conv_final = jnp.transpose(conv_final, (1, 0, 2))
     layer_out = expert_layer(
         gated,
         proj_out,
@@ -826,7 +865,7 @@
         expert_up,
         expert_down,
     )
-    return (layer_out.astype(BF16), conv_final, ssm_state)
+    return (finish(layer_out), conv_final, ssm_state)
 
 
 def solution(mesh):

time: 113 us -> 109 us (0.965)
  other arithmetic: 1.56 us -> 0 us
    convert_element_type x1 -> x0, other arithmetic: 1.56 us -> none  [shards(): return (layer_out.astype(BF16), conv_final, ssm_state)]
    pallas_call x0 -> x1, Pallas kernels: none -> 1.55 us  [finish(): pl.pallas_call(finish_kernel, out_shape=jax.ShapeDtypeStruct(value.shape,...]
where the time goes in v4:
time: 109 us
  Pallas kernels  109 us (100%)
    pallas_call x1, Pallas kernels, expert_layer(): pl.pallas_call(expert_kernel, out_shape=jax.ShapeDtypeStruct((2, 4, 4096)...  82 us
    pallas_call x1, Pallas kernels, mixer_in(): pl.pallas_call(mixer_in_kernel, out_shape=(jax.ShapeDtypeStruct((3, 128,...  21.4 us
    pallas_call x1, Pallas kernels, recurrence(): pl.pallas_call(recurrence_kernel, grid=(128 // BLOCK,), out_shape=(jax.Sh...  3.79 us

profile of v4, /device:TPU:1, one launch (start us, length us, event | category | flops | bytes accessed | tf_op | source)
XLA Modules:
  0.0 109.3 jit_solution(2126430414804925040)
XLA Ops:
  0.6 21.4 %mixer_in.1 = (bf16[3,128,128]{2,1,0:T(8,128)(2,1)}, bf16[256,128]{1,0:T(8,128)(2,1)}, f32[256,128]{1,0:T(8,128)}, f32[256,128]{1,0:T(8,128)}, bf16[256,64]{1,0:T(8,128)(2,1)}) custom-call(bf16[256,4096]{1,0:T(8,128)(2,1)} %bitcast.13, bf16[4096,128]{1,0:T(8,128)(2,1)} %inner_hbm.1, bf16[4096,128]{1,0:T(8,128)(2,1)} %gate_hbm.2, ...), custom_call_target="tpu_custom_call" | custom-call | tf_op jit(solution)/shard_map/mixer_in/pallas_call | solution.py:194
  22.0 3.8 %recurrence.1 = (bf16[2,128,128]{2,1,0:T(8,128)(2,1)}, f32[128,16,128]{2,1,0:T(8,128)}, bf16[3,128,128]{2,1,0:T(8,128)(2,1)}) custom-call(f32[2,128,128]{2,1,0:T(8,128)} %bitcast.15, bf16[2,128,128]{2,1,0:T(8,128)(2,1)} %bitcast.17, f32[2,128,128]{2,1,0:T(8,128)} %bitcast.14, bf16[2,128,64]{2,1,0:T(8,128)(2,1)} %bitcast.18, f32[16,128]{1,0:T(8,128)} %decay_log.1, ...), custom_call_target="tpu_custom_call" | custom-call | tf_op jit(solution)/shard_map/recurrence/pallas_call | solution.py:264
  25.8 82.0 %experts.1.value = f32[2,4,4096]{2,1,0:T(4,128)} custom-call(bf16[2,128,128]{2,1,0:T(8,128)(2,1)} %get-tuple-element.16.gated_hbm, bf16[128,4096]{1,0:T(8,128)(2,1)} %weight_hbm.1, s32[2,2,4]{2,1,0:T(2,128)} %bitcast.20, f32[2,2,4]{2,1,0:T(2,128)} %bitcast.21, bf16[2,128,4096]{2,1,0:T(8,128)(2,1)} %layer_hbm.1, bf16[1,512,4096]{2,1,0:T(8,128)(2,1)} %gate_hbm.3, ...), custom_call_target="tpu_custom_call" | custom-call | tf_op jit(solution)/shard_map/experts/pallas_call | solution.py:750
  107.8 1.6 %finish.1 = bf16[2,4,4096]{2,1,0:T(4,128)(2,1)} custom-call(f32[2,4,4096]{2,1,0:T(4,128)} %experts.1.value), custom_call_target="tpu_custom_call" | custom-call | tf_op jit(solution)/shard_map/finish/pallas_call | solution.py:805

commit v5 on v4

--- a/solution.py
+++ b/solution.py
@@ -703,8 +703,8 @@
     for load in loads[:2]:
         load.wait()
     compute(0, 0)
+    compute(0, 1)
     third10 = third_gather(1, 0, second1)
-    compute(0, 1)
     loads[2].wait()
     project(0, 0)
     hop00 = first_reduce(0, 0)

time: 109 us -> 108 us (level)
  no operation moved by 1% of the time
where the time goes in v5:
time: 108 us
  Pallas kernels  108 us (100%)
    pallas_call x1, Pallas kernels, expert_layer(): pl.pallas_call(expert_kernel, out_shape=jax.ShapeDtypeStruct((2, 4, 4096)...  80.9 us
    pallas_call x1, Pallas kernels, mixer_in(): pl.pallas_call(mixer_in_kernel, out_shape=(jax.ShapeDtypeStruct((3, 128,...  21.4 us
    pallas_call x1, Pallas kernels, recurrence(): pl.pallas_call(recurrence_kernel, grid=(128 // BLOCK,), out_shape=(jax.Sh...  3.79 us

profile of v5, /device:TPU:1, one launch (start us, length us, event | category | flops | bytes accessed | tf_op | source)
XLA Modules:
  0.0 108.2 jit_solution(1391485945223624843)
XLA Ops:
  0.6 21.4 %mixer_in.1 = (bf16[3,128,128]{2,1,0:T(8,128)(2,1)}, bf16[256,128]{1,0:T(8,128)(2,1)}, f32[256,128]{1,0:T(8,128)}, f32[256,128]{1,0:T(8,128)}, bf16[256,64]{1,0:T(8,128)(2,1)}) custom-call(bf16[256,4096]{1,0:T(8,128)(2,1)} %bitcast.13, bf16[4096,128]{1,0:T(8,128)(2,1)} %inner_hbm.1, bf16[4096,128]{1,0:T(8,128)(2,1)} %gate_hbm.2, ...), custom_call_target="tpu_custom_call" | custom-call | tf_op jit(solution)/shard_map/mixer_in/pallas_call | solution.py:194
  22.0 3.8 %recurrence.1 = (bf16[2,128,128]{2,1,0:T(8,128)(2,1)}, f32[128,16,128]{2,1,0:T(8,128)}, bf16[3,128,128]{2,1,0:T(8,128)(2,1)}) custom-call(f32[2,128,128]{2,1,0:T(8,128)} %bitcast.15, bf16[2,128,128]{2,1,0:T(8,128)(2,1)} %bitcast.17, f32[2,128,128]{2,1,0:T(8,128)} %bitcast.14, bf16[2,128,64]{2,1,0:T(8,128)(2,1)} %bitcast.18, f32[16,128]{1,0:T(8,128)} %decay_log.1, ...), custom_call_target="tpu_custom_call" | custom-call | tf_op jit(solution)/shard_map/recurrence/pallas_call | solution.py:264
  25.8 80.9 %experts.1.value = f32[2,4,4096]{2,1,0:T(4,128)} custom-call(bf16[2,128,128]{2,1,0:T(8,128)(2,1)} %get-tuple-element.16.gated_hbm, bf16[128,4096]{1,0:T(8,128)(2,1)} %weight_hbm.1, s32[2,2,4]{2,1,0:T(2,128)} %bitcast.20, f32[2,2,4]{2,1,0:T(2,128)} %bitcast.21, bf16[2,128,4096]{2,1,0:T(8,128)(2,1)} %layer_hbm.1, bf16[1,512,4096]{2,1,0:T(8,128)(2,1)} %gate_hbm.3, ...), custom_call_target="tpu_custom_call" | custom-call | tf_op jit(solution)/shard_map/experts/pallas_call | solution.py:750
  106.7 1.6 %finish.1 = bf16[2,4,4096]{2,1,0:T(4,128)(2,1)} custom-call(f32[2,4,4096]{2,1,0:T(4,128)} %experts.1.value), custom_call_target="tpu_custom_call" | custom-call | tf_op jit(solution)/shard_map/finish/pallas_call | solution.py:805
